TPU v7x, 32 devices: a whole 2x2x4 slice. The times are simulated.
32 devices in a mesh: phi: 4 (over x, core), eta: 8 (over z, y).
Axes of the slice: x: 2, y: 2, z: 4, core: 2. Of those that a mesh axis runs over, the one named last changes fastest.
Arguments:
- query: bfloat16 [192, 16384], P(None, ('phi', 'eta')), may hold values from -64 to 64
- key_rows: bfloat16 [192, 16384], P(None, ('phi', 'eta')), may hold values from -6 to 6
- value: bfloat16 [192, 16384], P(None, ('phi', 'eta')), may hold values from -6 to 6
- out_grad: bfloat16 [192, 16384], P(None, ('phi', 'eta')), may hold values from -6 to 6
- members: int32 [3, 128, 128], P(None, ('phi', 'eta')), may hold values from 0 to 16383, as said below
Outputs:
- query_grad: bfloat16 [192, 16384], P(None, ('phi', 'eta'))
- key_grad: bfloat16 [192, 16384], P(None, ('phi', 'eta'))
- value_grad: bfloat16 [192, 16384], P(None, ('phi', 'eta'))
Inputs may be any that keep to these rules, and one draw needn't show every extreme that they name: `members`: bucket i of every table is owned by device i // 4 in the order phi+eta, and point id j lies on device j // 512. In each table every point id appears exactly once. In one table a device's buckets hold at most 20 points of any one source device, and exactly 20 for some pairs of devices.
All inputs are finite; a program needn't handle non-finite values.
Results may differ from a plain program's by a relative error of at most 0.0097.
Values may be sent and summed in bfloat16 or wider, within the bound.
No kernel may reach another device: no remote copies, remote signals or barrier semaphores. Data moves between devices by JAX's collectives and lax.ppermute only.
A program may use at most 64 MiB of HBM per device.

v0:
```python
import functools

import jax
import jax.numpy as jnp
from jax import lax
from jax.experimental import pallas as pl
from jax.experimental.pallas import tpu as pltpu
from jax.sharding import PartitionSpec as P

HEADS = 8
AXES = ("phi", "eta")
LOG2E = 1.4426950408889634
VMEM_BYTES = 48 * 1024 * 1024


def dot(a, b, da, db):
    return lax.dot_general(a, b, (((da,), (db,)), ((), ())), preferred_element_type=jnp.float32)


def column_of(row):
    n = row.shape[1]
    diagonal = lax.broadcasted_iota(jnp.int32, (n, n), 0) == lax.broadcasted_iota(jnp.int32, (n, n), 1)
    return jnp.sum(jnp.where(diagonal, jnp.broadcast_to(row, (n, n)), 0.0), axis=1, keepdims=True)


def one_hot_rows(column, width):
    n = column.shape[0]
    places = lax.broadcasted_iota(jnp.int32, (n, width), 1).astype(jnp.float32)
    return jnp.where(column == places, 1.0, 0.0).astype(jnp.bfloat16)


def slots_of(lids_ref, points):
    group = lids_ref.shape[0]
    lids = lids_ref[...].astype(jnp.float32)
    return jnp.concatenate([one_hot_rows(column_of(lids[o : o + 1]), points) for o in range(group)], axis=0)


def pack_kernel(lids_ref, q_ref, k_ref, v_ref, g_ref, out_ref):
    group, rows, width = out_ref.shape
    features = jnp.concatenate([q_ref[...], k_ref[...], v_ref[...], g_ref[...]], axis=0)
    picks = slots_of(lids_ref, features.shape[1])
    packed = dot(picks, features, 1, 1)
    out_ref[...] = packed.astype(jnp.bfloat16).reshape(group, rows, width)


def fold_kernel(lids_ref, replies_ref, out_ref):
    group, rows, width = replies_ref.shape
    picks = slots_of(lids_ref, out_ref.shape[1])
    out_ref[...] = dot(replies_ref[...].reshape(group * rows, width), picks, 0, 0).astype(jnp.bfloat16)


def finish_kernel(lids_ref, replies_ref, other_ref, q_ref, k_ref, v_ref):
    group, rows, width = replies_ref.shape
    picks = slots_of(lids_ref, other_ref.shape[1])
    total = dot(replies_ref[...].reshape(group * rows, width), picks, 0, 0) + other_ref[...].astype(jnp.float32)
    total = total.astype(jnp.bfloat16)
    third = width // 3
    q_ref[...] = total[:third]
    k_ref[...] = total[third : 2 * third]
    v_ref[...] = total[2 * third :]


def attend_kernel(windows, codes_ref, own_ref, other_ref, out_own_ref, out_other_ref, feats_ref, grads_ref):
    group, rows, width4 = own_ref.shape
    feat = width4 // 4
    head_dim = feat // HEADS
    scale = head_dim**-0.5
    tables, points = codes_ref.shape
    buckets = points // 128
    pair = 2 * head_dim
    head_of = lax.broadcasted_iota(jnp.int32, (pair, 256), 0) // head_dim
    block_of = lax.broadcasted_iota(jnp.int32, (pair, 256), 1) // 128
    mask = jnp.where(head_of == block_of, 1.0, 0.0).astype(jnp.bfloat16)

    def blocked(part):
        return jnp.concatenate([part, part], axis=1) * mask

    out_own_ref[...] = jnp.zeros_like(out_own_ref)
    out_other_ref[...] = jnp.zeros_like(out_other_ref)
    for t in range(tables):
        low, high = windows[t]
        span = high - low
        slots = 2 * group * span
        codes = codes_ref[t : t + 1, :].astype(jnp.float32)
        columns = jnp.concatenate([column_of(codes[:, b * 128 : (b + 1) * 128]) for b in range(buckets)], axis=0)
        picks = one_hot_rows(columns, slots)
        arrived = jnp.concatenate(
            [ref[:, low:high, :].reshape(group * span, width4) for ref in (own_ref, other_ref)], axis=0
        )
        feats_ref[...] = dot(picks, arrived, 1, 0).T.astype(jnp.bfloat16)

        def bucket(b, carry):
            lanes = pl.ds(pl.multiple_of(b * 128, 128), 128)
            for h in range(HEADS // 2):
                at = h * pair
                q = feats_ref[at : at + pair, lanes]
                k = feats_ref[feat + at : feat + at + pair, lanes]
                v = feats_ref[2 * feat + at : 2 * feat + at + pair, lanes]
                g = feats_ref[3 * feat + at : 3 * feat + at + pair, lanes]
                k_wide = k.astype(jnp.float32)
                k_block = blocked(k)
                squares = k_wide * k_wide
                norms = [
                    (0.5 * scale * LOG2E) * jnp.sum(squares[i * head_dim : (i + 1) * head_dim], axis=0, keepdims=True)
                    for i in range(2)
                ]
                scores = dot(q, k_block, 0, 0)
                dprob = dot(g, blocked(v), 0, 0)
                probs_low, dscore_low, sums = [], [], []
                for i in range(2):
                    cols = slice(i * 128, (i + 1) * 128)
                    logits = scores[:, cols] * (scale * LOG2E) - norms[i]
                    logits = logits - jnp.max(logits, axis=1, keepdims=True)
                    expons = jnp.exp2(logits)
                    probs = expons * (1.0 / jnp.sum(expons, axis=1, keepdims=True))
                    delta = jnp.sum(probs * dprob[:, cols], axis=1, keepdims=True)
                    dscore = probs * (dprob[:, cols] - delta)
                    probs_low.append(probs.astype(jnp.bfloat16))
                    dscore_low.append(dscore.astype(jnp.bfloat16))
                    sums.append(jnp.broadcast_to(jnp.sum(dscore, axis=0, keepdims=True), (head_dim, 128)))
                dscore_wide = jnp.concatenate(dscore_low, axis=1)
                dscore_tall = jnp.concatenate(dscore_low, axis=0)
                probs_tall = jnp.concatenate(probs_low, axis=0)
                dq = scale * dot(k_block, dscore_wide, 1, 1)
                dk = scale * (dot(blocked(q), dscore_tall, 1, 0) - jnp.concatenate(sums, axis=0) * k_wide)
                dv = dot(blocked(g), probs_tall, 1, 0)
                grads_ref[at : at + pair, lanes] = dq.astype(jnp.bfloat16)
                grads_ref[feat + at : feat + at + pair, lanes] = dk.astype(jnp.bfloat16)
                grads_ref[2 * feat + at : 2 * feat + at + pair, lanes] = dv.astype(jnp.bfloat16)
            return carry

        lax.fori_loop(0, buckets, bucket, 0)
        grads = grads_ref[...]
        for part, ref in enumerate((out_own_ref, out_other_ref)):
            places = lax.broadcasted_iota(jnp.int32, (group * span, points), 0).astype(jnp.float32) + float(
                part * group * span
            )
            back = jnp.where(places == codes, 1.0, 0.0).astype(jnp.bfloat16)
            rows_back = dot(back, grads, 1, 1).astype(jnp.bfloat16).reshape(group, span, 3 * feat)
            ref[:, low:high, :] = ref[:, low:high, :] + rows_back


def call(kernel, out_shape, scratch=(), flops=0, moved=0):
    return pl.pallas_call(
        kernel,
        out_shape=out_shape,
        scratch_shapes=list(scratch),
        compiler_params=pltpu.CompilerParams(vmem_limit_bytes=VMEM_BYTES),
        cost_estimate=pl.CostEstimate(flops=flops, bytes_accessed=moved, transcendentals=0),
    )


def on_device(query, key_rows, value, out_grad, members):
    points = query.shape[1]
    feat = query.shape[0]
    tables = members.shape[0]
    phi, eta = lax.axis_size("phi"), lax.axis_size("eta")
    owners = phi * eta
    half = eta // 2
    group = phi * half
    capacity = 5 * points // (4 * owners)
    rows = -(-tables * capacity // 16) * 16
    windows = [
        (t * capacity // 16 * 16, -(-(t * capacity + capacity) // 16) * 16) for t in range(tables)
    ]
    halves = [[p * eta + h * half + e for p in range(phi) for e in range(half)] for h in range(2)]
    across = [(p * eta + e, p * eta + (e + half) % eta) for p in range(phi) for e in range(eta)]

    def exchange(chunks):
        return lax.all_to_all(chunks, AXES, 0, 0, tiled=True, axis_index_groups=halves)

    bf16 = jnp.bfloat16
    arrays = (query, key_rows, value, out_grad)
    copies = [lax.ppermute(array, AXES, across) for array in arrays]

    ids = members.reshape(tables, points)
    home, local = ids // points, ids % points
    position = jnp.arange(points, dtype=jnp.int32)
    same = home[:, :, None] == home[:, None, :]
    earlier = position[None, :, None] > position[None, None, :]
    rank = jnp.sum((same & earlier).astype(jnp.int32), axis=2)
    home_p, home_e = home // eta, home % eta
    part = (home_e // half != lax.axis_index("eta") // half).astype(jnp.int32)
    place = home_p * half + home_e % half
    table = jnp.arange(tables, dtype=jnp.int32)[:, None]
    slot = (place * 2 + part) * rows + table * capacity + rank
    slots = jnp.arange(group * 2 * rows, dtype=jnp.int32)
    match = slots[:, None] == slot.reshape(1, -1)
    wanted = jnp.sum(jnp.where(match, local.reshape(1, -1) + 1, 0), axis=1) - 1
    lids = exchange(wanted.reshape(group, 2, rows))
    lows = jnp.array([low for low, _ in windows], jnp.int32)[:, None]
    spans = jnp.array([high - low for low, high in windows], jnp.int32)[:, None]
    codes = (part * group + place) * spans + table * capacity + rank - lows

    packed = jax.ShapeDtypeStruct((group, rows, 4 * feat), bf16)
    reply = jax.ShapeDtypeStruct((group, rows, 3 * feat), bf16)
    column = jax.ShapeDtypeStruct((feat, points), bf16)
    pack = call(pack_kernel, packed, flops=2 * group * rows * points * 4 * feat, moved=2 * group * rows * 4 * feat)
    arrived_own = exchange(pack(lids[:, 0], *arrays))
    arrived_other = exchange(pack(lids[:, 1], *copies))
    attend = call(
        functools.partial(attend_kernel, windows),
        (reply, reply),
        scratch=(pltpu.VMEM((4 * feat, points), bf16), pltpu.VMEM((3 * feat, points), bf16)),
        flops=2 * 10**10,
        moved=8 * 10**6,
    )
    reply_own, reply_other = attend(codes, arrived_own, arrived_other)
    returned_other = exchange(reply_other)
    fold = call(
        fold_kernel,
        jax.ShapeDtypeStruct((3 * feat, points), bf16),
        flops=2 * group * rows * points * 3 * feat,
        moved=2 * group * rows * 3 * feat,
    )
    summed = lax.ppermute(fold(lids[:, 1], returned_other), AXES, across)
    returned_own = exchange(reply_own)
    finish = call(
        finish_kernel,
        (column, column, column),
        flops=2 * group * rows * points * 3 * feat,
        moved=2 * group * rows * 3 * feat,
    )
    return finish(lids[:, 0], returned_own, summed)


def solution(mesh):
    split = P(None, AXES)
    in_specs = (split, split, split, split, P(None, AXES, None))
    return jax.shard_map(
        on_device, mesh=mesh, in_specs=in_specs, out_specs=(split, split, split), check_vma=False
    )
```

profile of v0, /device:TPU:0, one launch (start us, length us, event | category | flops | bytes accessed | tf_op | source)
XLA Modules:
  0.0 181.4 jit_solution(1856760208119879943)
XLA Ops:
  0.8 0.7 reshape.219
  1.5 0.7 add_select_fusion.5
  2.2 1.0 convert_reduce_fusion
  3.3 1.3 select_reduce_fusion
  4.8 11.5 %all_to_all.25 = s32[16,1,128]{2,1,0:T(1,128)S(1)} all-to-all(s32[16,1,128]{2,1,0:T(1,128)S(1)} %reshape.221), channel_id=1, replica_groups={{0,1,2,3,8,9,10,11,16,17,18,19,24,25,26,27},{4,5,6,7,12,13,14,15,20,21,..., dimensions={0} | all-to-all | bytes 16384 | tf_op jit(solution)/shard_map/all_to_all | solution.py:170
  16.4 0.5 broadcast.296
  16.9 0.7 reduce
  17.7 0.9 copy-done.1
  18.6 0.9 copy-done.3
  19.5 0.9 copy-done.5
  20.4 0.9 copy-done.7
  21.4 2.2 %shard_map.94 = bf16[16,64,768]{2,1,0:T(8,128)(2,1)} custom-call(s32[16,64]{1,0:T(8,128)S(1)} %bitcast.27, bf16[192,512]{1,0:T(8,128)(2,1)S(1)} %copy-done.1, bf16[192,512]{1,0:T(8,128)(2,1)S(1)} %copy-done.3, bf16[192,512]{1,0:T(8,128)(2,1)S(1)} %copy-done.5, bf16[192,512]{1,0:T(8,128)(2,1)S(1)} %copy-done.7), custom_call_target="tpu_custom_call" | custom-call | flops 805306368 | bytes 1572864 | tf_op jit(solution)/shard_map/pallas_call | solution.py:199
  23.6 3.9 %all-to-all-start.1 = ((bf16[16,64,768]{2,1,0:T(8,128)(2,1)}), bf16[16,64,768]{2,1,0:T(8,128)(2,1)S(1)}, u32[]{:S(2)}, u32[]{:S(2)}) async-start(bf16[16,64,768]{2,1,0:T(8,128)(2,1)} %shard_map.94), calls=%async_computation.1 | async-start | bytes 3145728 | tf_op jit(solution)/shard_map/all_to_all | solution.py:170
  27.4 2.7 %collective-permute-start = (bf16[192,512]{1,0:T(8,128)(2,1)S(1)}, bf16[192,512]{1,0:T(8,128)(2,1)S(1)}, u32[]{:S(2)}, u32[]{:S(2)}) collective-permute-start(bf16[192,512]{1,0:T(8,128)(2,1)S(1)} %copy-done.2), channel_id=1, source_target_pairs={{0,4},{1,5},{2,6},{3,7},{4,0},{5,1},{6,2},{7,3},{8,12},{9,13},{10,... | collective-permute-start | bytes 589832 | tf_op jit(solution)/shard_map/ppermute | solution.py:174
  30.1 0.3 collective-permute-start.1
  30.4 2.6 %collective-permute-start.2 = (bf16[192,512]{1,0:T(8,128)(2,1)S(1)}, bf16[192,512]{1,0:T(8,128)(2,1)S(1)}, u32[]{:S(2)}, u32[]{:S(2)}) collective-permute-start(bf16[192,512]{1,0:T(8,128)(2,1)S(1)} %copy-done.6), channel_id=1, source_target_pairs={{0,4},{1,5},{2,6},{3,7},{4,0},{5,1},{6,2},{7,3},{8,12},{9,13},{10,... | collective-permute-start | bytes 589832 | tf_op jit(solution)/shard_map/ppermute | solution.py:174
  33.0 0.3 collective-permute-start.3
  33.4 16.7 %collective-permute-done.q_ref = bf16[192,512]{1,0:T(8,128)(2,1)S(1)} collective-permute-done((bf16[192,512]{1,0:T(8,128)(2,1)S(1)}, bf16[192,512]{1,0:T(8,128)(2,1)S(1)}, u32[]{:S(2)}, u32[]{:S(2)}) %collective-permute-start) | collective-permute-done | bytes 196640 | tf_op jit(solution)/shard_map/ppermute | solution.py:174
  50.0 4.2 %collective-permute-done.1.k_ref = bf16[192,512]{1,0:T(8,128)(2,1)S(1)} collective-permute-done((bf16[192,512]{1,0:T(8,128)(2,1)S(1)}, bf16[192,512]{1,0:T(8,128)(2,1)S(1)}, u32[]{:S(2)}, u32[]{:S(2)}) %collective-permute-start.1) | collective-permute-done | bytes 196640 | tf_op jit(solution)/shard_map/ppermute | solution.py:174
  54.3 4.2 %collective-permute-done.2.v_ref = bf16[192,512]{1,0:T(8,128)(2,1)S(1)} collective-permute-done((bf16[192,512]{1,0:T(8,128)(2,1)S(1)}, bf16[192,512]{1,0:T(8,128)(2,1)S(1)}, u32[]{:S(2)}, u32[]{:S(2)}) %collective-permute-start.2) | collective-permute-done | bytes 196640 | tf_op jit(solution)/shard_map/ppermute | solution.py:174
  58.5 3.9 %collective-permute-done.3.g_ref = bf16[192,512]{1,0:T(8,128)(2,1)S(1)} collective-permute-done((bf16[192,512]{1,0:T(8,128)(2,1)S(1)}, bf16[192,512]{1,0:T(8,128)(2,1)S(1)}, u32[]{:S(2)}, u32[]{:S(2)}) %collective-permute-start.3) | collective-permute-done | bytes 196640 | tf_op jit(solution)/shard_map/ppermute | solution.py:174
  62.4 2.2 %shard_map.95 = bf16[16,64,768]{2,1,0:T(8,128)(2,1)} custom-call(s32[16,64]{1,0:T(8,128)S(1)} %bitcast.29, bf16[192,512]{1,0:T(8,128)(2,1)S(1)} %collective-permute-done.q_ref, bf16[192,512]{1,0:T(8,128)(2,1)S(1)} %collective-permute-done.1.k_ref, bf16[192,512]{1,0:T(8,128)(2,1)S(1)} %collective-permute-done.2.v_ref, ...), custom_call_target="tpu_custom_call" | custom-call | flops 805306368 | bytes 1572864 | tf_op jit(solution)/shard_map/pallas_call | solution.py:200
  64.6 0.1 all-to-all-done.1.own_ref
  64.7 8.8 %all-to-all-start.2 = ((bf16[16,64,768]{2,1,0:T(8,128)(2,1)}), bf16[16,64,768]{2,1,0:T(8,128)(2,1)S(1)}, u32[]{:S(2)}, u32[]{:S(2)}) async-start(bf16[16,64,768]{2,1,0:T(8,128)(2,1)} %shard_map.95), calls=%async_computation.2 | async-start | bytes 3145728 | tf_op jit(solution)/shard_map/all_to_all | solution.py:170
  73.5 21.7 %all-to-all-done.2.other_ref = bf16[16,64,768]{2,1,0:T(8,128)(2,1)S(1)} async-done(((bf16[16,64,768]{2,1,0:T(8,128)(2,1)}), bf16[16,64,768]{2,1,0:T(8,128)(2,1)S(1)}, u32[]{:S(2)}, u32[]{:S(2)}) %all-to-all-start.2) | async-done | bytes 1572896 | tf_op jit(solution)/shard_map/all_to_all | solution.py:170
  95.3 28.8 %shard_map.96 = (bf16[16,64,576]{2,1,0:T(8,128)(2,1)S(1)}, bf16[16,64,576]{2,1,0:T(8,128)(2,1)S(1)}) custom-call(s32[3,512]{1,0:T(4,128)S(1)} %fusion.18.codes_ref, bf16[16,64,768]{2,1,0:T(8,128)(2,1)S(1)} %all-to-all-done.1.own_ref, bf16[16,64,768]{2,1,0:T(8,128)(2,1)S(1)} %all-to-all-done.2.other_ref), custom_call_target="tpu_custom_call" | custom-call | flops 20000000000 | bytes 8000000 | tf_op jit(solution)/shard_map/pallas_call | solution.py:208
  124.1 21.7 %all_to_all.26.replies_ref = bf16[16,64,576]{2,1,0:T(8,128)(2,1)S(1)} all-to-all(bf16[16,64,576]{2,1,0:T(8,128)(2,1)S(1)} %get-tuple-element.6), channel_id=1, replica_groups={{0,1,2,3,8,9,10,11,16,17,18,19,24,25,26,27},{4,5,6,7,12,13,14,15,20,21,..., dimensions={0} | all-to-all | bytes 2359296 | tf_op jit(solution)/shard_map/all_to_all | solution.py:170
  145.8 3.7 %all-to-all-start.3 = ((bf16[16,64,576]{2,1,0:T(8,128)(2,1)}), bf16[16,64,576]{2,1,0:T(8,128)(2,1)S(1)}, u32[]{:S(2)}, u32[]{:S(2)}) async-start(bf16[16,64,576]{2,1,0:T(8,128)(2,1)} %copy-done), calls=%async_computation.3 | async-start | bytes 2621440 | tf_op jit(solution)/shard_map/all_to_all | solution.py:170
  149.6 1.7 shard_map.97
  151.2 1.4 collective-permute-start.4
  152.6 27.1 %all-to-all-done.3.replies_ref = bf16[16,64,576]{2,1,0:T(8,128)(2,1)S(1)} async-done(((bf16[16,64,576]{2,1,0:T(8,128)(2,1)}), bf16[16,64,576]{2,1,0:T(8,128)(2,1)S(1)}, u32[]{:S(2)}, u32[]{:S(2)}) %all-to-all-start.3) | async-done | bytes 1179680 | tf_op jit(solution)/shard_map/all_to_all | solution.py:170
  179.8 1.6 shard_map.98
  (30 shorter events, 0.6 us)
Async XLA Ops:
  17.6 0.9 copy-start.1
  18.6 0.9 copy-start.3
  19.5 0.9 copy-start.5
  20.4 0.9 copy-start.7
  23.6 3.9 %copy-start.2 = (bf16[192,512]{1,0:T(8,128)(2,1)S(1)}, bf16[192,512]{1,0:T(8,128)(2,1)}, u32[]{:S(2)}) copy-start(bf16[192,512]{1,0:T(8,128)(2,1)} %q_ref.1) | copy-start | bytes 589828
  23.6 6.5 %copy-start.4 = (bf16[192,512]{1,0:T(8,128)(2,1)S(1)}, bf16[192,512]{1,0:T(8,128)(2,1)}, u32[]{:S(2)}) copy-start(bf16[192,512]{1,0:T(8,128)(2,1)} %k_ref.1) | copy-start | bytes 589828
  23.6 6.9 %copy-start.6 = (bf16[192,512]{1,0:T(8,128)(2,1)S(1)}, bf16[192,512]{1,0:T(8,128)(2,1)}, u32[]{:S(2)}) copy-start(bf16[192,512]{1,0:T(8,128)(2,1)} %v_ref.1) | copy-start | bytes 589828
  23.6 9.5 %copy-start.8 = (bf16[192,512]{1,0:T(8,128)(2,1)S(1)}, bf16[192,512]{1,0:T(8,128)(2,1)}, u32[]{:S(2)}) copy-start(bf16[192,512]{1,0:T(8,128)(2,1)} %g_ref.1) | copy-start | bytes 589828
  23.6 41.1 %all-to-all-start.1 = ((bf16[16,64,768]{2,1,0:T(8,128)(2,1)}), bf16[16,64,768]{2,1,0:T(8,128)(2,1)S(1)}, u32[]{:S(2)}, u32[]{:S(2)}) async-start(bf16[16,64,768]{2,1,0:T(8,128)(2,1)} %shard_map.94), calls=%async_computation.1 | async-start | bytes 3145728 | tf_op jit(solution)/shard_map/all_to_all | solution.py:170
  27.4 22.6 %collective-permute-start = (bf16[192,512]{1,0:T(8,128)(2,1)S(1)}, bf16[192,512]{1,0:T(8,128)(2,1)S(1)}, u32[]{:S(2)}, u32[]{:S(2)}) collective-permute-start(bf16[192,512]{1,0:T(8,128)(2,1)S(1)} %copy-done.2), channel_id=1, source_target_pairs={{0,4},{1,5},{2,6},{3,7},{4,0},{5,1},{6,2},{7,3},{8,12},{9,13},{10,... | collective-permute-start | bytes 589832 | tf_op jit(solution)/shard_map/ppermute | solution.py:174
  30.1 24.2 %collective-permute-start.1 = (bf16[192,512]{1,0:T(8,128)(2,1)S(1)}, bf16[192,512]{1,0:T(8,128)(2,1)S(1)}, u32[]{:S(2)}, u32[]{:S(2)}) collective-permute-start(bf16[192,512]{1,0:T(8,128)(2,1)S(1)} %copy-done.4), channel_id=1, source_target_pairs={{0,4},{1,5},{2,6},{3,7},{4,0},{5,1},{6,2},{7,3},{8,12},{9,13},{10,... | collective-permute-start | bytes 589832 | tf_op jit(solution)/shard_map/ppermute | solution.py:174
  30.4 28.0 %collective-permute-start.2 = (bf16[192,512]{1,0:T(8,128)(2,1)S(1)}, bf16[192,512]{1,0:T(8,128)(2,1)S(1)}, u32[]{:S(2)}, u32[]{:S(2)}) collective-permute-start(bf16[192,512]{1,0:T(8,128)(2,1)S(1)} %copy-done.6), channel_id=1, source_target_pairs={{0,4},{1,5},{2,6},{3,7},{4,0},{5,1},{6,2},{7,3},{8,12},{9,13},{10,... | collective-permute-start | bytes 589832 | tf_op jit(solution)/shard_map/ppermute | solution.py:174
  33.0 29.4 %collective-permute-start.3 = (bf16[192,512]{1,0:T(8,128)(2,1)S(1)}, bf16[192,512]{1,0:T(8,128)(2,1)S(1)}, u32[]{:S(2)}, u32[]{:S(2)}) collective-permute-start(bf16[192,512]{1,0:T(8,128)(2,1)S(1)} %copy-done.8), channel_id=1, source_target_pairs={{0,4},{1,5},{2,6},{3,7},{4,0},{5,1},{6,2},{7,3},{8,12},{9,13},{10,... | collective-permute-start | bytes 589832 | tf_op jit(solution)/shard_map/ppermute | solution.py:174
  64.6 8.9 %copy-start.9 = (s32[3,4,128]{2,1,0:T(4,128)S(1)}, s32[3,4,128]{2,1,0:T(4,128)}, u32[]{:S(2)}) copy-start(s32[3,4,128]{2,1,0:T(4,128)} %param.11) | copy-start | bytes 18436
  64.7 30.6 %all-to-all-start.2 = ((bf16[16,64,768]{2,1,0:T(8,128)(2,1)}), bf16[16,64,768]{2,1,0:T(8,128)(2,1)S(1)}, u32[]{:S(2)}, u32[]{:S(2)}) async-start(bf16[16,64,768]{2,1,0:T(8,128)(2,1)} %shard_map.95), calls=%async_computation.2 | async-start | bytes 3145728 | tf_op jit(solution)/shard_map/all_to_all | solution.py:170
  124.1 21.7 %copy-start = (bf16[16,64,576]{2,1,0:T(8,128)(2,1)}, bf16[16,64,576]{2,1,0:T(8,128)(2,1)S(1)}, u32[]{:S(2)}) copy-start(bf16[16,64,576]{2,1,0:T(8,128)(2,1)S(1)} %get-tuple-element.5) | copy-start | bytes 3538948
  145.8 33.9 %all-to-all-start.3 = ((bf16[16,64,576]{2,1,0:T(8,128)(2,1)}), bf16[16,64,576]{2,1,0:T(8,128)(2,1)S(1)}, u32[]{:S(2)}, u32[]{:S(2)}) async-start(bf16[16,64,576]{2,1,0:T(8,128)(2,1)} %copy-done), calls=%async_computation.3 | async-start | bytes 2621440 | tf_op jit(solution)/shard_map/all_to_all | solution.py:170
  151.2 28.6 %collective-permute-start.4 = (bf16[576,512]{1,0:T(8,128)(2,1)}, bf16[576,512]{1,0:T(8,128)(2,1)S(1)}, u32[]{:S(2)}, u32[]{:S(2)}) collective-permute-start(bf16[576,512]{1,0:T(8,128)(2,1)} %shard_map.97), channel_id=1, source_target_pairs={{0,4},{1,5},{2,6},{3,7},{4,0},{5,1},{6,2},{7,3},{8,12},{9,13},{10,... | collective-permute-start | bytes 1769480 | tf_op jit(solution)/shard_map/ppermute | solution.py:216
where the time goes:
time: 182 us; the launch traced here: 181 us
  waiting for transfers between devices  78 us (43%)
  Pallas kernels  36.4 us (20%)
  blocking collectives  33.2 us (18%)
  starting transfers between devices  23.6 us (13%)
  local copies, waits for them, and re-layouts  5.29 us (3%)
  other arithmetic  3.91 us (2%)
    all_to_all x3, waiting for transfers between devices, exchange(): lax.all_to_all(chunks, AXES, 0, 0, tiled=True, axis_index_groups=halves)  49 us
    all_to_all x2, blocking collectives, exchange(): lax.all_to_all(chunks, AXES, 0, 0, tiled=True, axis_index_groups=halves)  33.2 us
    ppermute x4, waiting for transfers between devices, on_device(): copies = [lax.ppermute(array, AXES, across) for array in arrays]  29 us
    pallas_call x1, Pallas kernels, on_device(): reply_own, reply_other = attend(codes, arrived_own, arrived_other)  28.8 us
    all_to_all x3, starting transfers between devices, exchange(): lax.all_to_all(chunks, AXES, 0, 0, tiled=True, axis_index_groups=halves)  16.3 us
    ppermute x4, starting transfers between devices, on_device(): copies = [lax.ppermute(array, AXES, across) for array in arrays]  5.91 us
    unnamed x22, local copies, waits for them, and re-layouts  3.89 us
  transfers between devices with their start and end apart: 8, of which 7 were waited for; matrix products, arithmetic and copies ran while one was open for 0% of the time, Pallas kernels for 2%

commit v1 on v0

v1 whole, which is shorter than its diff:
```python
import functools

import jax
import jax.numpy as jnp
from jax import lax
from jax.experimental import pallas as pl
from jax.experimental.pallas import tpu as pltpu
from jax.sharding import PartitionSpec as P

HEADS = 8
BUCKET = 128
AXES = ("phi", "eta")
LOG2E = 1.4426950408889634
VMEM_BYTES = 48 * 1024 * 1024
PACK_FLOPS = 4 * 10**10


def dot(a, b, da, db):
    return lax.dot_general(a, b, (((da,), (db,)), ((), ())), preferred_element_type=jnp.float32)


def column_of(row, first, count):
    n = row.shape[1]
    diagonal = lax.broadcasted_iota(jnp.int32, (count, n), 0) + first == lax.broadcasted_iota(jnp.int32, (count, n), 1)
    return jnp.sum(jnp.where(diagonal, jnp.broadcast_to(row, (count, n)), 0.0), axis=1, keepdims=True)


def slots_of(wanted_ref, part, rows, points):
    group = wanted_ref.shape[0]
    wanted = wanted_ref[...].astype(jnp.float32)
    places = lax.broadcasted_iota(jnp.int32, (rows, points), 1).astype(jnp.float32)
    picks = [
        jnp.where(column_of(wanted[o, :1], part * rows, rows) == places, 1.0, 0.0).astype(jnp.bfloat16)
        for o in range(group)
    ]
    return jnp.concatenate(picks, axis=0)


def index_kernel(sizes, half_ref, members_ref, wanted_ref, codes_ref):
    windows, capacity, rows, eta = sizes
    tables, buckets, _ = members_ref.shape
    points = buckets * BUCKET
    group = wanted_ref.shape[0]
    half = eta // 2
    f32, bf16 = jnp.float32, jnp.bfloat16
    ids = jnp.concatenate([members_ref[:, b, :] for b in range(buckets)], axis=1).astype(f32)
    home = jnp.floor((ids + 0.5) * (1.0 / points))
    local = ids - home * points
    home_p = jnp.floor((home + 0.5) * (1.0 / eta))
    home_e = home - home_p * eta
    home_h = jnp.floor((home_e + 0.5) * (1.0 / half))
    part = jnp.where(home_h == half_ref[0, 0].astype(f32), 0.0, 1.0)
    place = home_p * half + home_e - home_h * half
    before = lax.broadcasted_iota(jnp.int32, (points, points), 0) < lax.broadcasted_iota(jnp.int32, (points, points), 1)
    before = jnp.where(before, 1.0, 0.0).astype(bf16)
    homes = lax.broadcasted_iota(jnp.int32, (2 * group, points), 0).astype(f32)
    holders = lax.broadcasted_iota(jnp.int32, (group, points), 0).astype(f32)
    lanes = lax.broadcasted_iota(jnp.int32, (2 * rows, points), 0).astype(f32)
    total = jnp.zeros((2 * group, 2 * rows), f32)
    for t in range(tables):
        row = slice(t, t + 1)
        hot = jnp.where(homes == home[row], 1.0, 0.0)
        rank = jnp.sum(hot * dot(hot.astype(bf16), before, 1, 0), axis=0, keepdims=True)
        slot = rank + float(t * capacity)
        low, high = windows[t]
        code = (part[row] * float(group) + place[row]) * float(high - low) + slot - float(low)
        codes_ref[row, :] = code.astype(jnp.int32)
        named = local[row] + 1.0
        large = jnp.floor(named * (1.0 / 256.0)) * 256.0
        held = holders == place[row]
        values = jnp.concatenate([jnp.where(held, large, 0.0), jnp.where(held, named - large, 0.0)], axis=0)
        at = jnp.where(lanes == part[row] * float(rows) + slot, 1.0, 0.0)
        total += dot(values.astype(bf16), at.astype(bf16), 1, 1)
    wanted = (total[:group] + total[group:] - 1.0).astype(jnp.int32)
    for o in range(group):
        wanted_ref[o] = jnp.broadcast_to(wanted[o : o + 1], wanted_ref.shape[1:])


def pack_kernel(part, wanted_ref, q_ref, k_ref, v_ref, g_ref, out_ref, features_ref, sems):
    group, rows, width = out_ref.shape
    feat, points = q_ref.shape
    copies = [
        pltpu.make_async_copy(ref, features_ref.at[pl.ds(n * feat, feat)], sems.at[n])
        for n, ref in enumerate((q_ref, k_ref, v_ref, g_ref))
    ]
    for copy in copies:
        copy.start()
    picks = slots_of(wanted_ref, part, rows, points)
    for copy in copies:
        copy.wait()
    packed = dot(picks, features_ref[...], 1, 1)
    out_ref[...] = packed.astype(jnp.bfloat16).reshape(group, rows, width)


def fold_kernel(wanted_ref, replies_ref, out_ref):
    group, rows, width = replies_ref.shape
    picks = slots_of(wanted_ref, 1, rows, out_ref.shape[1])
    out_ref[...] = dot(replies_ref[...].reshape(group * rows, width), picks, 0, 0).astype(jnp.bfloat16)


def finish_kernel(wanted_ref, replies_ref, other_ref, q_ref, k_ref, v_ref):
    group, rows, width = replies_ref.shape
    picks = slots_of(wanted_ref, 0, rows, other_ref.shape[1])
    total = dot(replies_ref[...].reshape(group * rows, width), picks, 0, 0) + other_ref[...].astype(jnp.float32)
    total = total.astype(jnp.bfloat16)
    third = width // 3
    q_ref[...] = total[:third]
    k_ref[...] = total[third : 2 * third]
    v_ref[...] = total[2 * third :]


def attend_kernel(
    windows,
    codes_ref,
    own_ref,
    other_ref,
    out_own_ref,
    out_other_ref,
    feats_ref,
    grads_ref,
    scores_ref,
    dprobs_ref,
    probs_ref,
    dscores_ref,
    falls_ref,
):
    group, rows, width4 = own_ref.shape
    feat = width4 // 4
    head_dim = feat // HEADS
    scale = head_dim**-0.5
    tables, points = codes_ref.shape
    buckets = points // BUCKET
    pair = 2 * head_dim
    bf16 = jnp.bfloat16
    head_of = lax.broadcasted_iota(jnp.int32, (pair, 2 * BUCKET), 0) // head_dim
    block_of = lax.broadcasted_iota(jnp.int32, (pair, 2 * BUCKET), 1) // BUCKET
    mask = jnp.where(head_of == block_of, 1.0, 0.0).astype(bf16)
    tail = lax.broadcasted_iota(jnp.int32, (16, BUCKET), 0)
    tail_wide = lax.broadcasted_iota(jnp.int32, (16, 2 * BUCKET), 0)
    tail_block = lax.broadcasted_iota(jnp.int32, (16, 2 * BUCKET), 1) // BUCKET
    halves = jnp.where((tail_wide < 6) & (tail_wide // 3 == tail_block), -0.5, 0.0).astype(bf16)
    lane = lax.broadcasted_iota(jnp.int32, (BUCKET, BUCKET), 1)

    def blocked(part):
        return jnp.concatenate([part, part], axis=1) * mask

    def norm_rows(k):
        wide = k.astype(jnp.float32)
        squares = wide * wide
        first, second = (
            jnp.sum(squares[i * head_dim : (i + 1) * head_dim], axis=0, keepdims=True) for i in range(2)
        )
        norm = jnp.where(tail < 3, first, second)
        high = norm.astype(bf16).astype(jnp.float32)
        rest = norm - high
        middle = rest.astype(bf16).astype(jnp.float32)
        piece = tail % 3
        out = jnp.where(piece == 0, high, jnp.where(piece == 1, middle, rest - middle))
        return jnp.where(tail < 6, out, 0.0).astype(bf16)

    out_own_ref[...] = jnp.zeros_like(out_own_ref)
    out_other_ref[...] = jnp.zeros_like(out_other_ref)
    todo = [(b, h) for b in range(buckets) for h in range(HEADS // 2)]
    for t in range(tables):
        low, high = windows[t]
        span = high - low
        slots = 2 * group * span
        codes = codes_ref[t : t + 1, :].astype(jnp.float32)
        places = lax.broadcasted_iota(jnp.int32, (slots, points), 0).astype(jnp.float32)
        picks = jnp.where(places == codes, 1.0, 0.0).astype(bf16)
        arrived = jnp.concatenate(
            [ref[:, low:high, :].reshape(group * span, width4) for ref in (own_ref, other_ref)], axis=0
        )
        feats_ref[...] = dot(arrived, picks, 0, 0).astype(bf16)

        def part_of(which, b, h):
            at = which * feat + h * pair
            return feats_ref[at : at + pair, b * BUCKET : (b + 1) * BUCKET]

        for n, (b, h) in enumerate(todo):
            q, k, v, g = (part_of(which, b, h) for which in range(4))
            scores_ref[n] = dot(
                jnp.concatenate([k, norm_rows(k)], axis=0), jnp.concatenate([blocked(q), halves], axis=0), 0, 0
            )
            dprobs_ref[n] = dot(v, blocked(g), 0, 0)
        for n in range(len(todo)):
            for i in range(2):
                cols = slice(i * BUCKET, (i + 1) * BUCKET)
                dprob = dprobs_ref[n, :, cols]
                scores = scores_ref[n, :, cols]
                expons = jnp.exp2((scores - jnp.max(scores, axis=0, keepdims=True)) * (scale * LOG2E))
                probs = expons * (1.0 / jnp.sum(expons, axis=0, keepdims=True))
                delta = jnp.sum(probs * dprob, axis=0, keepdims=True)
                dscore = probs * (dprob - delta)
                probs_ref[n, :, cols] = probs.astype(bf16)
                dscores_ref[n, :, cols] = dscore.astype(bf16)
                falls_ref[n, i] = jnp.broadcast_to(jnp.sum(dscore, axis=1, keepdims=True), (BUCKET, BUCKET))
        for n, (b, h) in enumerate(todo):
            if h == 0:
                falls = sum(
                    jnp.where(lane == i, falls_ref[b * (HEADS // 2) + i // 2, i % 2], 0.0) for i in range(HEADS)
                ).T
            q, k, g = (part_of(which, b, h) for which in (0, 1, 3))
            dscore_tall = jnp.concatenate([dscores_ref[n, :, :BUCKET], dscores_ref[n, :, BUCKET:]], axis=0)
            dq = scale * dot(blocked(k), dscore_tall, 1, 0)
            fall = jnp.concatenate(
                [jnp.broadcast_to(falls[i : i + 1], (head_dim, BUCKET)) for i in (2 * h, 2 * h + 1)], axis=0
            )
            dk = scale * (dot(blocked(q), dscores_ref[n], 1, 1) - fall * k.astype(jnp.float32))
            dv = dot(blocked(g), probs_ref[n], 1, 1)
            for which, grad in enumerate((dq, dk, dv)):
                at = which * feat + h * pair
                grads_ref[at : at + pair, b * BUCKET : (b + 1) * BUCKET] = grad.astype(bf16)
        back = dot(picks, grads_ref[...], 1, 1).astype(bf16).reshape(2, group, span, 3 * feat)
        for part, ref in enumerate((out_own_ref, out_other_ref)):
            ref[:, low:high, :] = ref[:, low:high, :] + back[part]


def call(kernel, out_shape, scratch=(), flops=0, moved=0, in_specs=None):
    extra = {} if in_specs is None else {"in_specs": in_specs}
    return pl.pallas_call(
        kernel,
        out_shape=out_shape,
        scratch_shapes=list(scratch),
        compiler_params=pltpu.CompilerParams(vmem_limit_bytes=VMEM_BYTES),
        cost_estimate=pl.CostEstimate(flops=flops, bytes_accessed=moved, transcendentals=0),
        **extra,
    )


def on_device(query, key_rows, value, out_grad, members):
    feat, points = query.shape
    tables = members.shape[0]
    phi, eta = lax.axis_size("phi"), lax.axis_size("eta")
    half = eta // 2
    group = phi * half
    capacity = 5 * points // (4 * phi * eta)
    rows = -(-tables * capacity // 16) * 16
    windows = [(t * capacity // 16 * 16, -(-(t * capacity + capacity) // 16) * 16) for t in range(tables)]
    halves = [[p * eta + h * half + e for p in range(phi) for e in range(half)] for h in range(2)]
    across = [(p * eta + e, p * eta + (e + half) % eta) for p in range(phi) for e in range(eta)]
    bf16 = jnp.bfloat16
    packed = jax.ShapeDtypeStruct((group, rows, 4 * feat), bf16)
    reply = jax.ShapeDtypeStruct((group, rows, 3 * feat), bf16)
    column = jax.ShapeDtypeStruct((feat, points), bf16)
    steps = points // BUCKET * (HEADS // 2)
    vmem = pl.BlockSpec(memory_space=pltpu.VMEM)

    def exchange(chunks):
        return lax.all_to_all(chunks, AXES, 0, 0, tiled=True, axis_index_groups=halves)

    def pack(part, flops):
        return call(
            functools.partial(pack_kernel, part),
            packed,
            scratch=(pltpu.VMEM((4 * feat, points), bf16), pltpu.SemaphoreType.DMA((4,))),
            in_specs=[vmem] + [pl.BlockSpec(memory_space=pltpu.HBM)] * 4,
            flops=flops,
            moved=2 * group * rows * 4 * feat,
        )

    arrays = (query, key_rows, value, out_grad)
    copies = [lax.ppermute(array, AXES, across) for array in arrays]

    index = call(
        functools.partial(index_kernel, (windows, capacity, rows, eta)),
        (
            jax.ShapeDtypeStruct((group, 8, 2 * rows), jnp.int32),
            jax.ShapeDtypeStruct((tables, points), jnp.int32),
        ),
        in_specs=[pl.BlockSpec(memory_space=pltpu.SMEM), vmem],
        flops=10**9,
        moved=10**5,
    )
    wanted, codes = index((lax.axis_index("eta") // half).astype(jnp.int32).reshape(1, 1), members)
    wanted = exchange(wanted)

    arrived_own = exchange(pack(0, 2 * group * rows * points * 4 * feat)(wanted, *arrays))
    arrived_other = exchange(pack(1, PACK_FLOPS)(wanted, *copies))
    attend = call(
        functools.partial(attend_kernel, windows),
        (reply, reply),
        scratch=(
            pltpu.VMEM((4 * feat, points), bf16),
            pltpu.VMEM((3 * feat, points), bf16),
            pltpu.VMEM((steps, BUCKET, 2 * BUCKET), jnp.float32),
            pltpu.VMEM((steps, BUCKET, 2 * BUCKET), jnp.float32),
            pltpu.VMEM((steps, BUCKET, 2 * BUCKET), bf16),
            pltpu.VMEM((steps, BUCKET, 2 * BUCKET), bf16),
            pltpu.VMEM((steps, 2, BUCKET, BUCKET), jnp.float32),
        ),
        flops=2 * 10**10,
        moved=8 * 10**6,
    )
    reply_own, reply_other = attend(codes, arrived_own, arrived_other)
    returned_other = exchange(reply_other)
    fold = call(
        fold_kernel,
        jax.ShapeDtypeStruct((3 * feat, points), bf16),
        flops=2 * group * rows * points * 3 * feat,
        moved=2 * group * rows * 3 * feat,
    )
    folded, reply_own = lax.optimization_barrier((fold(wanted, returned_other), reply_own))
    summed = lax.ppermute(folded, AXES, across)
    returned_own = exchange(reply_own)
    finish = call(
        finish_kernel,
        (column, column, column),
        flops=2 * group * rows * points * 3 * feat,
        moved=2 * group * rows * 3 * feat,
    )
    return finish(wanted, returned_own, summed)


def solution(mesh):
    split = P(None, AXES)
    in_specs = (split, split, split, split, P(None, AXES, None))
    return jax.shard_map(
        on_device, mesh=mesh, in_specs=in_specs, out_specs=(split, split, split), check_vma=False
    )
```

time: 182 us -> 155 us (0.85)
  waiting for transfers between devices: 78 us -> 54.6 us
  Pallas kernels: 36.4 us -> 21.6 us
  blocking collectives: 33.2 us -> 45.9 us
  other arithmetic: 3.91 us -> 0 us
    all_to_all x3, waiting for transfers between devices: 49 us -> 9.08 us  [exchange(): lax.all_to_all(chunks, AXES, 0, 0, tiled=True, axis_index_groups=halves)]
    ppermute x1, waiting for transfers between devices: 0.01 us -> 23.6 us  [on_device(): summed = lax.ppermute(folded, AXES, across)]
    pallas_call x1, Pallas kernels: 28.8 us -> 12.2 us  [on_device(): reply_own, reply_other = attend(codes, arrived_own, arrived_other)]
    all_to_all x2, blocking collectives: 33.2 us -> 45.9 us  [exchange(): lax.all_to_all(chunks, AXES, 0, 0, tiled=True, axis_index_groups=halves)]
    ppermute x4, waiting for transfers between devices: 29 us -> 22 us  [on_device(): copies = [lax.ppermute(array, AXES, across) for array in arrays]]
    ppermute x1, starting transfers between devices: 1.42 us -> 4.17 us  [on_device(): summed = lax.ppermute(folded, AXES, across)]
    reduce_sum x2 -> x0, other arithmetic: 2.34 us -> none  [the longest x1 1.33 us: on_device(): wanted = jnp.sum(jnp.where(match, local.reshape(1, -1) + 1, 0), axis=1) - 1]
    pallas_call x4 -> x5, Pallas kernels: 7.62 us -> 9.43 us  [the longest x1 3.42 us: on_device(): pack(0, 2 * group * rows * points * 4 * feat)(wanted, *arrays)]
  transfers between devices with their start and end apart: 8 -> 8, of which waited for: 7 -> 7; matrix products, arithmetic and copies ran while one was open for 0% -> 0% of each run, Pallas kernels for 2% -> 4%
where the time goes in v1:
time: 155 us; the launch traced here: 154 us
  waiting for transfers between devices  54.6 us (35%)
  blocking collectives  45.9 us (30%)
  starting transfers between devices  25.2 us (16%)
  Pallas kernels  21.6 us (14%)
  local copies, waits for them, and re-layouts  5.51 us (4%)
    all_to_all x2, blocking collectives, exchange(): lax.all_to_all(chunks, AXES, 0, 0, tiled=True, axis_index_groups=halves)  45.9 us
    ppermute x1, waiting for transfers between devices, on_device(): summed = lax.ppermute(folded, AXES, across)  23.6 us
    ppermute x4, waiting for transfers between devices, on_device(): copies = [lax.ppermute(array, AXES, across) for array in arrays]  22 us
    all_to_all x3, starting transfers between devices, exchange(): lax.all_to_all(chunks, AXES, 0, 0, tiled=True, axis_index_groups=halves)  15.1 us
    pallas_call x1, Pallas kernels, on_device(): reply_own, reply_other = attend(codes, arrived_own, arrived_other)  12.2 us
    all_to_all x3, waiting for transfers between devices, exchange(): lax.all_to_all(chunks, AXES, 0, 0, tiled=True, axis_index_groups=halves)  9.08 us
    ppermute x4, starting transfers between devices, on_device(): copies = [lax.ppermute(array, AXES, across) for array in arrays]  5.91 us
    unnamed x22, local copies, waits for them, and re-layouts  5.51 us
  transfers between devices with their start and end apart: 8, of which 7 were waited for; matrix products, arithmetic and copies ran while one was open for 0% of the time, Pallas kernels for 4%

profile of v1, /device:TPU:0, one launch (start us, length us, event | category | flops | bytes accessed | tf_op | source)
XLA Modules:
  0.0 153.6 jit_solution(10799558216773526291)
XLA Ops:
  0.7 0.7 copy-done.10
  1.3 1.3 shard_map.76
  2.7 6.3 %all-to-all-start = ((s32[16,8,128]{2,1,0:T(8,128)}), s32[16,8,128]{2,1,0:T(8,128)S(1)}, u32[]{:S(2)}, u32[]{:S(2)}) async-start(s32[16,8,128]{2,1,0:T(8,128)} %get-tuple-element.9), calls=%async_computation | async-start | bytes 131072 | tf_op jit(solution)/shard_map/all_to_all | solution.py:250
  9.0 2.7 %collective-permute-start = (bf16[192,512]{1,0:T(8,128)(2,1)S(1)}, bf16[192,512]{1,0:T(8,128)(2,1)S(1)}, u32[]{:S(2)}, u32[]{:S(2)}) collective-permute-start(bf16[192,512]{1,0:T(8,128)(2,1)S(1)} %copy-done), channel_id=1, source_target_pairs={{0,4},{1,5},{2,6},{3,7},{4,0},{5,1},{6,2},{7,3},{8,12},{9,13},{10,... | collective-permute-start | bytes 589832 | tf_op jit(solution)/shard_map/ppermute | solution.py:263
  11.7 0.3 collective-permute-start.1
  12.0 2.6 %collective-permute-start.2 = (bf16[192,512]{1,0:T(8,128)(2,1)S(1)}, bf16[192,512]{1,0:T(8,128)(2,1)S(1)}, u32[]{:S(2)}, u32[]{:S(2)}) collective-permute-start(bf16[192,512]{1,0:T(8,128)(2,1)S(1)} %copy-done.2), channel_id=1, source_target_pairs={{0,4},{1,5},{2,6},{3,7},{4,0},{5,1},{6,2},{7,3},{8,12},{9,13},{10,... | collective-permute-start | bytes 589832 | tf_op jit(solution)/shard_map/ppermute | solution.py:263
  14.6 0.0 copy-done.3
  14.6 0.3 collective-permute-start.3
  14.9 0.0 all-to-all-done.wanted_ref
  14.9 3.4 %shard_map.77 = bf16[16,64,768]{2,1,0:T(8,128)(2,1)} custom-call(s32[16,8,128]{2,1,0:T(8,128)S(1)} %all-to-all-done.wanted_ref, bf16[192,512]{1,0:T(8,128)(2,1)S(1)} %copy-done, bf16[192,512]{1,0:T(8,128)(2,1)S(1)} %copy-done.1, bf16[192,512]{1,0:T(8,128)(2,1)S(1)} %copy-done.2, bf16[192,512]{1,0:T(8,128)(2,1)S(1)} %copy-done.3), custom_call_target="tpu_custom_call" | custom-call | flops 805306368 | bytes 1572864 | tf_op jit(solution)/shard_map/pallas_call | solution.py:278
  18.4 5.1 %all-to-all-start.1 = ((bf16[16,64,768]{2,1,0:T(8,128)(2,1)}), bf16[16,64,768]{2,1,0:T(8,128)(2,1)S(1)}, u32[]{:S(2)}, u32[]{:S(2)}) async-start(bf16[16,64,768]{2,1,0:T(8,128)(2,1)} %shard_map.77), calls=%async_computation.1 | async-start | bytes 3145728 | tf_op jit(solution)/shard_map/all_to_all | solution.py:250
  23.5 11.1 %collective-permute-done.q_ref = bf16[192,512]{1,0:T(8,128)(2,1)S(1)} collective-permute-done((bf16[192,512]{1,0:T(8,128)(2,1)S(1)}, bf16[192,512]{1,0:T(8,128)(2,1)S(1)}, u32[]{:S(2)}, u32[]{:S(2)}) %collective-permute-start) | collective-permute-done | bytes 196640 | tf_op jit(solution)/shard_map/ppermute | solution.py:263
  34.6 4.2 %collective-permute-done.1.k_ref = bf16[192,512]{1,0:T(8,128)(2,1)S(1)} collective-permute-done((bf16[192,512]{1,0:T(8,128)(2,1)S(1)}, bf16[192,512]{1,0:T(8,128)(2,1)S(1)}, u32[]{:S(2)}, u32[]{:S(2)}) %collective-permute-start.1) | collective-permute-done | bytes 196640 | tf_op jit(solution)/shard_map/ppermute | solution.py:263
  38.8 0.7 copy-done.4
  39.5 3.5 %collective-permute-done.2.v_ref = bf16[192,512]{1,0:T(8,128)(2,1)S(1)} collective-permute-done((bf16[192,512]{1,0:T(8,128)(2,1)S(1)}, bf16[192,512]{1,0:T(8,128)(2,1)S(1)}, u32[]{:S(2)}, u32[]{:S(2)}) %collective-permute-start.2) | collective-permute-done | bytes 196640 | tf_op jit(solution)/shard_map/ppermute | solution.py:263
  43.1 0.7 copy-done.6
  43.7 3.1 %collective-permute-done.3.g_ref = bf16[192,512]{1,0:T(8,128)(2,1)S(1)} collective-permute-done((bf16[192,512]{1,0:T(8,128)(2,1)S(1)}, bf16[192,512]{1,0:T(8,128)(2,1)S(1)}, u32[]{:S(2)}, u32[]{:S(2)}) %collective-permute-start.3) | collective-permute-done | bytes 196640 | tf_op jit(solution)/shard_map/ppermute | solution.py:263
  46.8 0.7 copy-done.8
  47.5 0.9 copy-done.5
  48.4 0.9 copy-done.7
  49.3 0.9 copy-done.9
  50.3 2.2 %shard_map.78 = bf16[16,64,768]{2,1,0:T(8,128)(2,1)S(1)} custom-call(s32[16,8,128]{2,1,0:T(8,128)S(1)} %all-to-all-done.wanted_ref, bf16[192,512]{1,0:T(8,128)(2,1)S(1)} %collective-permute-done.q_ref, bf16[192,512]{1,0:T(8,128)(2,1)S(1)} %copy-done.5, bf16[192,512]{1,0:T(8,128)(2,1)S(1)} %copy-done.7, bf16[192,512]{1,0:T(8,128)(2,1)S(1)} %copy-done.9), custom_call_target="tpu_custom_call" | custom-call | flops 40000000000 | bytes 1572864 | tf_op jit(solution)/shard_map/pallas_call | solution.py:279
  52.5 6.6 %all-to-all-done.1.own_ref = bf16[16,64,768]{2,1,0:T(8,128)(2,1)S(1)} async-done(((bf16[16,64,768]{2,1,0:T(8,128)(2,1)}), bf16[16,64,768]{2,1,0:T(8,128)(2,1)S(1)}, u32[]{:S(2)}, u32[]{:S(2)}) %all-to-all-start.1) | async-done | bytes 1572896 | tf_op jit(solution)/shard_map/all_to_all | solution.py:250
  59.1 24.8 %all_to_all.25.other_ref = bf16[16,64,768]{2,1,0:T(8,128)(2,1)S(1)} all-to-all(bf16[16,64,768]{2,1,0:T(8,128)(2,1)S(1)} %shard_map.78), channel_id=1, replica_groups={{0,1,2,3,8,9,10,11,16,17,18,19,24,25,26,27},{4,5,6,7,12,13,14,15,20,21,..., dimensions={0} | all-to-all | bytes 3145728 | tf_op jit(solution)/shard_map/all_to_all | solution.py:250
  83.9 12.2 %shard_map.79 = (bf16[16,64,576]{2,1,0:T(8,128)(2,1)}, bf16[16,64,576]{2,1,0:T(8,128)(2,1)S(1)}) custom-call(s32[3,512]{1,0:T(4,128)S(1)} %get-tuple-element.10.codes_ref, bf16[16,64,768]{2,1,0:T(8,128)(2,1)S(1)} %all-to-all-done.1.own_ref, bf16[16,64,768]{2,1,0:T(8,128)(2,1)S(1)} %all_to_all.25.other_ref), custom_call_target="tpu_custom_call" | custom-call | flops 20000000000 | bytes 8000000 | tf_op jit(solution)/shard_map/pallas_call | solution.py:295
  96.1 21.1 %all_to_all.26.replies_ref = bf16[16,64,576]{2,1,0:T(8,128)(2,1)S(1)} all-to-all(bf16[16,64,576]{2,1,0:T(8,128)(2,1)S(1)} %get-tuple-element.11), channel_id=1, replica_groups={{0,1,2,3,8,9,10,11,16,17,18,19,24,25,26,27},{4,5,6,7,12,13,14,15,20,21,..., dimensions={0} | all-to-all | bytes 2359296 | tf_op jit(solution)/shard_map/all_to_all | solution.py:250
  117.2 0.9 shard_map.80
  118.1 3.7 %all-to-all-start.4 = ((bf16[16,64,576]{2,1,0:T(8,128)(2,1)}), bf16[16,64,576]{2,1,0:T(8,128)(2,1)S(1)}, u32[]{:S(2)}, u32[]{:S(2)}) async-start(bf16[16,64,576]{2,1,0:T(8,128)(2,1)} %get-tuple-element.13), calls=%async_computation.4 | async-start | bytes 2621440 | tf_op jit(solution)/shard_map/all_to_all | solution.py:250
  121.8 4.2 %collective-permute-start.4 = (bf16[576,512]{1,0:T(8,128)(2,1)S(1)}, bf16[576,512]{1,0:T(8,128)(2,1)S(1)}, u32[]{:S(2)}, u32[]{:S(2)}) collective-permute-start(bf16[576,512]{1,0:T(8,128)(2,1)S(1)} %shard_map.80), channel_id=1, source_target_pairs={{0,4},{1,5},{2,6},{3,7},{4,0},{5,1},{6,2},{7,3},{8,12},{9,13},{10,... | collective-permute-start | bytes 1769480 | tf_op jit(solution)/shard_map/ppermute | solution.py:304
  126.0 23.6 %collective-permute-done.4.other_ref = bf16[576,512]{1,0:T(8,128)(2,1)S(1)} collective-permute-done((bf16[576,512]{1,0:T(8,128)(2,1)S(1)}, bf16[576,512]{1,0:T(8,128)(2,1)S(1)}, u32[]{:S(2)}, u32[]{:S(2)}) %collective-permute-start.4) | collective-permute-done | bytes 589856 | tf_op jit(solution)/shard_map/ppermute | solution.py:304
  149.5 2.5 %all-to-all-done.4.replies_ref = bf16[16,64,576]{2,1,0:T(8,128)(2,1)S(1)} async-done(((bf16[16,64,576]{2,1,0:T(8,128)(2,1)}), bf16[16,64,576]{2,1,0:T(8,128)(2,1)S(1)}, u32[]{:S(2)}, u32[]{:S(2)}) %all-to-all-start.4) | async-done | bytes 1179680 | tf_op jit(solution)/shard_map/all_to_all | solution.py:250
  152.0 1.6 %shard_map.81 = (bf16[192,512]{1,0:T(8,128)(2,1)}, bf16[192,512]{1,0:T(8,128)(2,1)}, bf16[192,512]{1,0:T(8,128)(2,1)}) custom-call(s32[16,8,128]{2,1,0:T(8,128)S(1)} %all-to-all-done.wanted_ref, bf16[16,64,576]{2,1,0:T(8,128)(2,1)S(1)} %all-to-all-done.4.replies_ref, bf16[576,512]{1,0:T(8,128)(2,1)S(1)} %collective-permute-done.4.other_ref), custom_call_target="tpu_custom_call" | custom-call | flops 603979776 | bytes 1179648 | tf_op jit(solution)/shard_map/pallas_call | solution.py:312
  (14 shorter events, 0.0 us)
Async XLA Ops:
  0.6 0.7 copy-start.10
  1.3 7.7 %copy-start = (bf16[192,512]{1,0:T(8,128)(2,1)S(1)}, bf16[192,512]{1,0:T(8,128)(2,1)}, u32[]{:S(2)}) copy-start(bf16[192,512]{1,0:T(8,128)(2,1)} %q_ref.1) | copy-start | bytes 589828
  1.3 10.3 %copy-start.1 = (bf16[192,512]{1,0:T(8,128)(2,1)S(1)}, bf16[192,512]{1,0:T(8,128)(2,1)}, u32[]{:S(2)}) copy-start(bf16[192,512]{1,0:T(8,128)(2,1)} %k_ref.1) | copy-start | bytes 589828
  1.3 10.7 %copy-start.2 = (bf16[192,512]{1,0:T(8,128)(2,1)S(1)}, bf16[192,512]{1,0:T(8,128)(2,1)}, u32[]{:S(2)}) copy-start(bf16[192,512]{1,0:T(8,128)(2,1)} %v_ref.1) | copy-start | bytes 589828
  1.3 13.2 %copy-start.3 = (bf16[192,512]{1,0:T(8,128)(2,1)S(1)}, bf16[192,512]{1,0:T(8,128)(2,1)}, u32[]{:S(2)}) copy-start(bf16[192,512]{1,0:T(8,128)(2,1)} %g_ref.1) | copy-start | bytes 589828
  2.7 12.2 %all-to-all-start = ((s32[16,8,128]{2,1,0:T(8,128)}), s32[16,8,128]{2,1,0:T(8,128)S(1)}, u32[]{:S(2)}, u32[]{:S(2)}) async-start(s32[16,8,128]{2,1,0:T(8,128)} %get-tuple-element.9), calls=%async_computation | async-start | bytes 131072 | tf_op jit(solution)/shard_map/all_to_all | solution.py:250
  9.0 25.6 %collective-permute-start = (bf16[192,512]{1,0:T(8,128)(2,1)S(1)}, bf16[192,512]{1,0:T(8,128)(2,1)S(1)}, u32[]{:S(2)}, u32[]{:S(2)}) collective-permute-start(bf16[192,512]{1,0:T(8,128)(2,1)S(1)} %copy-done), channel_id=1, source_target_pairs={{0,4},{1,5},{2,6},{3,7},{4,0},{5,1},{6,2},{7,3},{8,12},{9,13},{10,... | collective-permute-start | bytes 589832 | tf_op jit(solution)/shard_map/ppermute | solution.py:263
  11.7 27.2 %collective-permute-start.1 = (bf16[192,512]{1,0:T(8,128)(2,1)S(1)}, bf16[192,512]{1,0:T(8,128)(2,1)S(1)}, u32[]{:S(2)}, u32[]{:S(2)}) collective-permute-start(bf16[192,512]{1,0:T(8,128)(2,1)S(1)} %copy-done.1), channel_id=1, source_target_pairs={{0,4},{1,5},{2,6},{3,7},{4,0},{5,1},{6,2},{7,3},{8,12},{9,13},{10,... | collective-permute-start | bytes 589832 | tf_op jit(solution)/shard_map/ppermute | solution.py:263
  12.0 31.1 %collective-permute-start.2 = (bf16[192,512]{1,0:T(8,128)(2,1)S(1)}, bf16[192,512]{1,0:T(8,128)(2,1)S(1)}, u32[]{:S(2)}, u32[]{:S(2)}) collective-permute-start(bf16[192,512]{1,0:T(8,128)(2,1)S(1)} %copy-done.2), channel_id=1, source_target_pairs={{0,4},{1,5},{2,6},{3,7},{4,0},{5,1},{6,2},{7,3},{8,12},{9,13},{10,... | collective-permute-start | bytes 589832 | tf_op jit(solution)/shard_map/ppermute | solution.py:263
  14.6 32.2 %collective-permute-start.3 = (bf16[192,512]{1,0:T(8,128)(2,1)S(1)}, bf16[192,512]{1,0:T(8,128)(2,1)S(1)}, u32[]{:S(2)}, u32[]{:S(2)}) collective-permute-start(bf16[192,512]{1,0:T(8,128)(2,1)S(1)} %copy-done.3), channel_id=1, source_target_pairs={{0,4},{1,5},{2,6},{3,7},{4,0},{5,1},{6,2},{7,3},{8,12},{9,13},{10,... | collective-permute-start | bytes 589832 | tf_op jit(solution)/shard_map/ppermute | solution.py:263
  18.4 40.7 %all-to-all-start.1 = ((bf16[16,64,768]{2,1,0:T(8,128)(2,1)}), bf16[16,64,768]{2,1,0:T(8,128)(2,1)S(1)}, u32[]{:S(2)}, u32[]{:S(2)}) async-start(bf16[16,64,768]{2,1,0:T(8,128)(2,1)} %shard_map.77), calls=%async_computation.1 | async-start | bytes 3145728 | tf_op jit(solution)/shard_map/all_to_all | solution.py:250
  38.8 0.7 copy-start.4
  43.1 0.7 copy-start.6
  46.8 0.7 copy-start.8
  47.5 0.9 copy-start.5
  48.4 0.9 copy-start.7
  49.3 0.9 copy-start.9
  118.1 34.0 %all-to-all-start.4 = ((bf16[16,64,576]{2,1,0:T(8,128)(2,1)}), bf16[16,64,576]{2,1,0:T(8,128)(2,1)S(1)}, u32[]{:S(2)}, u32[]{:S(2)}) async-start(bf16[16,64,576]{2,1,0:T(8,128)(2,1)} %get-tuple-element.13), calls=%async_computation.4 | async-start | bytes 2621440 | tf_op jit(solution)/shard_map/all_to_all | solution.py:250
  121.8 27.7 %collective-permute-start.4 = (bf16[576,512]{1,0:T(8,128)(2,1)S(1)}, bf16[576,512]{1,0:T(8,128)(2,1)S(1)}, u32[]{:S(2)}, u32[]{:S(2)}) collective-permute-start(bf16[576,512]{1,0:T(8,128)(2,1)S(1)} %shard_map.80), channel_id=1, source_target_pairs={{0,4},{1,5},{2,6},{3,7},{4,0},{5,1},{6,2},{7,3},{8,12},{9,13},{10,... | collective-permute-start | bytes 1769480 | tf_op jit(solution)/shard_map/ppermute | solution.py:304

commit v2 on v1

--- a/solution.py
+++ b/solution.py
@@ -50,7 +50,9 @@
     home_e = home - home_p * eta
     home_h = jnp.floor((home_e + 0.5) * (1.0 / half))
     part = jnp.where(home_h == half_ref[0, 0].astype(f32), 0.0, 1.0)
-    place = home_p * half + home_e - home_h * half
+    within = home_e - home_h * half
+    deep = jnp.floor((within + 0.5) * (2.0 / half))
+    place = home_p * half + within + part * (0.5 * half) * (1.0 - 2.0 * deep)
     before = lax.broadcasted_iota(jnp.int32, (points, points), 0) < lax.broadcasted_iota(jnp.int32, (points, points), 1)
     before = jnp.where(before, 1.0, 0.0).astype(bf16)
     homes = lax.broadcasted_iota(jnp.int32, (2 * group, points), 0).astype(f32)
@@ -238,7 +240,10 @@
     rows = -(-tables * capacity // 16) * 16
     windows = [(t * capacity // 16 * 16, -(-(t * capacity + capacity) // 16) * 16) for t in range(tables)]
     halves = [[p * eta + h * half + e for p in range(phi) for e in range(half)] for h in range(2)]
-    across = [(p * eta + e, p * eta + (e + half) % eta) for p in range(phi) for e in range(eta)]
+    layer = eta // 4
+    across = [
+        (p * eta + z * layer + e, p * eta + (3 - z) * layer + e) for p in range(phi) for z in range(4) for e in range(layer)
+    ]
     bf16 = jnp.bfloat16
     packed = jax.ShapeDtypeStruct((group, rows, 4 * feat), bf16)
     reply = jax.ShapeDtypeStruct((group, rows, 3 * feat), bf16)

time: 155 us -> 149 us (0.961)
  waiting for transfers between devices: 54.6 us -> 46.6 us
  blocking collectives: 45.9 us -> 49.4 us
    ppermute x4, waiting for transfers between devices: 22 us -> 6.46 us  [on_device(): copies = [lax.ppermute(array, AXES, across) for array in arrays]]
    ppermute x1, waiting for transfers between devices: 23.6 us -> 28.6 us  [on_device(): summed = lax.ppermute(folded, AXES, across)]
    all_to_all x2, blocking collectives: 45.9 us -> 49.4 us  [exchange(): lax.all_to_all(chunks, AXES, 0, 0, tiled=True, axis_index_groups=halves)]
    all_to_all x3, waiting for transfers between devices: 9.08 us -> 11.6 us  [exchange(): lax.all_to_all(chunks, AXES, 0, 0, tiled=True, axis_index_groups=halves)]
    ppermute x4, starting transfers between devices: 5.91 us -> 7.92 us  [on_device(): copies = [lax.ppermute(array, AXES, across) for array in arrays]]
  transfers between devices with their start and end apart: 8 -> 8, of which waited for: 7 -> 4; matrix products, arithmetic and copies ran while one was open for 0% -> 0% of each run, Pallas kernels for 4% -> 4%
where the time goes in v2:
time: 149 us
  blocking collectives  49.4 us (33%)
  waiting for transfers between devices  46.6 us (31%)
  starting transfers between devices  24.9 us (17%)
  Pallas kernels  21.6 us (14%)
  local copies, waits for them, and re-layouts  5.5 us (4%)
    all_to_all x2, blocking collectives, exchange(): lax.all_to_all(chunks, AXES, 0, 0, tiled=True, axis_index_groups=halves)  49.4 us
    ppermute x1, waiting for transfers between devices, on_device(): summed = lax.ppermute(folded, AXES, across)  28.6 us
    all_to_all x3, starting transfers between devices, exchange(): lax.all_to_all(chunks, AXES, 0, 0, tiled=True, axis_index_groups=halves)  14 us
    pallas_call x1, Pallas kernels, on_device(): reply_own, reply_other = attend(codes, arrived_own, arrived_other)  12.2 us
    all_to_all x3, waiting for transfers between devices, exchange(): lax.all_to_all(chunks, AXES, 0, 0, tiled=True, axis_index_groups=halves)  11.6 us
    ppermute x4, starting transfers between devices, on_device(): copies = [lax.ppermute(array, AXES, across) for array in arrays]  7.92 us
    ppermute x4, waiting for transfers between devices, on_device(): copies = [lax.ppermute(array, AXES, across) for array in arrays]  6.46 us
    unnamed x22, local copies, waits for them, and re-layouts  5.5 us
  transfers between devices with their start and end apart: 8, of which 4 were waited for; matrix products, arithmetic and copies ran while one was open for 0% of the time, Pallas kernels for 4%

profile of v2, /device:TPU:0, one launch (start us, length us, event | category | flops | bytes accessed | tf_op | source)
XLA Modules:
  0.0 148.8 jit_solution(13074780500285267084)
XLA Ops:
  0.7 0.7 copy-done.10
  1.3 1.3 shard_map.76
  2.7 6.3 %all-to-all-start = ((s32[16,8,128]{2,1,0:T(8,128)}), s32[16,8,128]{2,1,0:T(8,128)S(1)}, u32[]{:S(2)}, u32[]{:S(2)}) async-start(s32[16,8,128]{2,1,0:T(8,128)} %get-tuple-element.9), calls=%async_computation | async-start | bytes 131072 | tf_op jit(solution)/shard_map/all_to_all | solution.py:255
  9.0 4.0 %collective-permute-start = (bf16[192,512]{1,0:T(8,128)(2,1)S(1)}, bf16[192,512]{1,0:T(8,128)(2,1)S(1)}, u32[]{:S(2)}, u32[]{:S(2)}) collective-permute-start(bf16[192,512]{1,0:T(8,128)(2,1)S(1)} %copy-done), channel_id=1, source_target_pairs={{0,6},{1,7},{2,4},{3,5},{4,2},{5,3},{6,0},{7,1},{8,14},{9,15},{10,... | collective-permute-start | bytes 589832 | tf_op jit(solution)/shard_map/ppermute | solution.py:268
  13.0 0.1 collective-permute-start.1
  13.1 3.7 %collective-permute-start.2 = (bf16[192,512]{1,0:T(8,128)(2,1)S(1)}, bf16[192,512]{1,0:T(8,128)(2,1)S(1)}, u32[]{:S(2)}, u32[]{:S(2)}) collective-permute-start(bf16[192,512]{1,0:T(8,128)(2,1)S(1)} %copy-done.2), channel_id=1, source_target_pairs={{0,6},{1,7},{2,4},{3,5},{4,2},{5,3},{6,0},{7,1},{8,14},{9,15},{10,... | collective-permute-start | bytes 589832 | tf_op jit(solution)/shard_map/ppermute | solution.py:268
  16.8 0.1 collective-permute-start.3
  16.9 0.0 all-to-all-done.wanted_ref
  16.9 3.4 %shard_map.77 = bf16[16,64,768]{2,1,0:T(8,128)(2,1)} custom-call(s32[16,8,128]{2,1,0:T(8,128)S(1)} %all-to-all-done.wanted_ref, bf16[192,512]{1,0:T(8,128)(2,1)S(1)} %copy-done, bf16[192,512]{1,0:T(8,128)(2,1)S(1)} %copy-done.1, bf16[192,512]{1,0:T(8,128)(2,1)S(1)} %copy-done.2, bf16[192,512]{1,0:T(8,128)(2,1)S(1)} %copy-done.3), custom_call_target="tpu_custom_call" | custom-call | flops 805306368 | bytes 1572864 | tf_op jit(solution)/shard_map/pallas_call | solution.py:283
  20.4 4.0 %all-to-all-start.1 = ((bf16[16,64,768]{2,1,0:T(8,128)(2,1)}), bf16[16,64,768]{2,1,0:T(8,128)(2,1)S(1)}, u32[]{:S(2)}, u32[]{:S(2)}) async-start(bf16[16,64,768]{2,1,0:T(8,128)(2,1)} %shard_map.77), calls=%async_computation.1 | async-start | bytes 3145728 | tf_op jit(solution)/shard_map/all_to_all | solution.py:255
  24.4 0.0 collective-permute-done.q_ref
  24.4 0.0 collective-permute-done.1.k_ref
  24.4 0.0 copy-start.4
  24.4 0.7 copy-done.4
  25.1 3.0 %collective-permute-done.2.v_ref = bf16[192,512]{1,0:T(8,128)(2,1)S(1)} collective-permute-done((bf16[192,512]{1,0:T(8,128)(2,1)S(1)}, bf16[192,512]{1,0:T(8,128)(2,1)S(1)}, u32[]{:S(2)}, u32[]{:S(2)}) %collective-permute-start.2) | collective-permute-done | bytes 196640 | tf_op jit(solution)/shard_map/ppermute | solution.py:268
  28.1 0.7 copy-done.6
  28.7 3.5 %collective-permute-done.3.g_ref = bf16[192,512]{1,0:T(8,128)(2,1)S(1)} collective-permute-done((bf16[192,512]{1,0:T(8,128)(2,1)S(1)}, bf16[192,512]{1,0:T(8,128)(2,1)S(1)}, u32[]{:S(2)}, u32[]{:S(2)}) %collective-permute-start.3) | collective-permute-done | bytes 196640 | tf_op jit(solution)/shard_map/ppermute | solution.py:268
  32.2 0.7 copy-done.8
  32.9 0.9 copy-done.5
  33.8 0.9 copy-done.7
  34.7 0.9 copy-done.9
  35.7 2.2 %shard_map.78 = bf16[16,64,768]{2,1,0:T(8,128)(2,1)S(1)} custom-call(s32[16,8,128]{2,1,0:T(8,128)S(1)} %all-to-all-done.wanted_ref, bf16[192,512]{1,0:T(8,128)(2,1)S(1)} %collective-permute-done.q_ref, bf16[192,512]{1,0:T(8,128)(2,1)S(1)} %copy-done.5, bf16[192,512]{1,0:T(8,128)(2,1)S(1)} %copy-done.7, bf16[192,512]{1,0:T(8,128)(2,1)S(1)} %copy-done.9), custom_call_target="tpu_custom_call" | custom-call | flops 40000000000 | bytes 1572864 | tf_op jit(solution)/shard_map/pallas_call | solution.py:284
  37.9 11.6 %all-to-all-done.1.own_ref = bf16[16,64,768]{2,1,0:T(8,128)(2,1)S(1)} async-done(((bf16[16,64,768]{2,1,0:T(8,128)(2,1)}), bf16[16,64,768]{2,1,0:T(8,128)(2,1)S(1)}, u32[]{:S(2)}, u32[]{:S(2)}) %all-to-all-start.1) | async-done | bytes 1572896 | tf_op jit(solution)/shard_map/all_to_all | solution.py:255
  49.5 28.3 %all_to_all.25.other_ref = bf16[16,64,768]{2,1,0:T(8,128)(2,1)S(1)} all-to-all(bf16[16,64,768]{2,1,0:T(8,128)(2,1)S(1)} %shard_map.78), channel_id=1, replica_groups={{0,1,2,3,8,9,10,11,16,17,18,19,24,25,26,27},{4,5,6,7,12,13,14,15,20,21,..., dimensions={0} | all-to-all | bytes 3145728 | tf_op jit(solution)/shard_map/all_to_all | solution.py:255
  77.8 12.2 %shard_map.79 = (bf16[16,64,576]{2,1,0:T(8,128)(2,1)}, bf16[16,64,576]{2,1,0:T(8,128)(2,1)S(1)}) custom-call(s32[3,512]{1,0:T(4,128)S(1)} %get-tuple-element.10.codes_ref, bf16[16,64,768]{2,1,0:T(8,128)(2,1)S(1)} %all-to-all-done.1.own_ref, bf16[16,64,768]{2,1,0:T(8,128)(2,1)S(1)} %all_to_all.25.other_ref), custom_call_target="tpu_custom_call" | custom-call | flops 20000000000 | bytes 8000000 | tf_op jit(solution)/shard_map/pallas_call | solution.py:300
  90.0 21.1 %all_to_all.26.replies_ref = bf16[16,64,576]{2,1,0:T(8,128)(2,1)S(1)} all-to-all(bf16[16,64,576]{2,1,0:T(8,128)(2,1)S(1)} %get-tuple-element.11), channel_id=1, replica_groups={{0,1,2,3,8,9,10,11,16,17,18,19,24,25,26,27},{4,5,6,7,12,13,14,15,20,21,..., dimensions={0} | all-to-all | bytes 2359296 | tf_op jit(solution)/shard_map/all_to_all | solution.py:255
  111.1 0.9 shard_map.80
  112.0 3.7 %all-to-all-start.4 = ((bf16[16,64,576]{2,1,0:T(8,128)(2,1)}), bf16[16,64,576]{2,1,0:T(8,128)(2,1)S(1)}, u32[]{:S(2)}, u32[]{:S(2)}) async-start(bf16[16,64,576]{2,1,0:T(8,128)(2,1)} %get-tuple-element.13), calls=%async_computation.4 | async-start | bytes 2621440 | tf_op jit(solution)/shard_map/all_to_all | solution.py:255
  115.7 2.9 %collective-permute-start.4 = (bf16[576,512]{1,0:T(8,128)(2,1)S(1)}, bf16[576,512]{1,0:T(8,128)(2,1)S(1)}, u32[]{:S(2)}, u32[]{:S(2)}) collective-permute-start(bf16[576,512]{1,0:T(8,128)(2,1)S(1)} %shard_map.80), channel_id=1, source_target_pairs={{0,6},{1,7},{2,4},{3,5},{4,2},{5,3},{6,0},{7,1},{8,14},{9,15},{10,... | collective-permute-start | bytes 1769480 | tf_op jit(solution)/shard_map/ppermute | solution.py:309
  118.6 28.6 %collective-permute-done.4.other_ref = bf16[576,512]{1,0:T(8,128)(2,1)S(1)} collective-permute-done((bf16[576,512]{1,0:T(8,128)(2,1)S(1)}, bf16[576,512]{1,0:T(8,128)(2,1)S(1)}, u32[]{:S(2)}, u32[]{:S(2)}) %collective-permute-start.4) | collective-permute-done | bytes 589856 | tf_op jit(solution)/shard_map/ppermute | solution.py:309
  147.2 0.0 all-to-all-done.4.replies_ref
  147.2 1.6 %shard_map.81 = (bf16[192,512]{1,0:T(8,128)(2,1)}, bf16[192,512]{1,0:T(8,128)(2,1)}, bf16[192,512]{1,0:T(8,128)(2,1)}) custom-call(s32[16,8,128]{2,1,0:T(8,128)S(1)} %all-to-all-done.wanted_ref, bf16[16,64,576]{2,1,0:T(8,128)(2,1)S(1)} %all-to-all-done.4.replies_ref, bf16[576,512]{1,0:T(8,128)(2,1)S(1)} %collective-permute-done.4.other_ref), custom_call_target="tpu_custom_call" | custom-call | flops 603979776 | bytes 1179648 | tf_op jit(solution)/shard_map/pallas_call | solution.py:317
  (14 shorter events, 0.0 us)
Async XLA Ops:
  0.6 0.7 copy-start.10
  1.3 7.7 %copy-start = (bf16[192,512]{1,0:T(8,128)(2,1)S(1)}, bf16[192,512]{1,0:T(8,128)(2,1)}, u32[]{:S(2)}) copy-start(bf16[192,512]{1,0:T(8,128)(2,1)} %q_ref.1) | copy-start | bytes 589828
  1.3 11.7 %copy-start.1 = (bf16[192,512]{1,0:T(8,128)(2,1)S(1)}, bf16[192,512]{1,0:T(8,128)(2,1)}, u32[]{:S(2)}) copy-start(bf16[192,512]{1,0:T(8,128)(2,1)} %k_ref.1) | copy-start | bytes 589828
  1.3 11.8 %copy-start.2 = (bf16[192,512]{1,0:T(8,128)(2,1)S(1)}, bf16[192,512]{1,0:T(8,128)(2,1)}, u32[]{:S(2)}) copy-start(bf16[192,512]{1,0:T(8,128)(2,1)} %v_ref.1) | copy-start | bytes 589828
  1.3 15.5 %copy-start.3 = (bf16[192,512]{1,0:T(8,128)(2,1)S(1)}, bf16[192,512]{1,0:T(8,128)(2,1)}, u32[]{:S(2)}) copy-start(bf16[192,512]{1,0:T(8,128)(2,1)} %g_ref.1) | copy-start | bytes 589828
  2.7 14.2 %all-to-all-start = ((s32[16,8,128]{2,1,0:T(8,128)}), s32[16,8,128]{2,1,0:T(8,128)S(1)}, u32[]{:S(2)}, u32[]{:S(2)}) async-start(s32[16,8,128]{2,1,0:T(8,128)} %get-tuple-element.9), calls=%async_computation | async-start | bytes 131072 | tf_op jit(solution)/shard_map/all_to_all | solution.py:255
  9.0 15.4 %collective-permute-start = (bf16[192,512]{1,0:T(8,128)(2,1)S(1)}, bf16[192,512]{1,0:T(8,128)(2,1)S(1)}, u32[]{:S(2)}, u32[]{:S(2)}) collective-permute-start(bf16[192,512]{1,0:T(8,128)(2,1)S(1)} %copy-done), channel_id=1, source_target_pairs={{0,6},{1,7},{2,4},{3,5},{4,2},{5,3},{6,0},{7,1},{8,14},{9,15},{10,... | collective-permute-start | bytes 589832 | tf_op jit(solution)/shard_map/ppermute | solution.py:268
  13.0 11.4 %collective-permute-start.1 = (bf16[192,512]{1,0:T(8,128)(2,1)S(1)}, bf16[192,512]{1,0:T(8,128)(2,1)S(1)}, u32[]{:S(2)}, u32[]{:S(2)}) collective-permute-start(bf16[192,512]{1,0:T(8,128)(2,1)S(1)} %copy-done.1), channel_id=1, source_target_pairs={{0,6},{1,7},{2,4},{3,5},{4,2},{5,3},{6,0},{7,1},{8,14},{9,15},{10,... | collective-permute-start | bytes 589832 | tf_op jit(solution)/shard_map/ppermute | solution.py:268
  13.1 15.0 %collective-permute-start.2 = (bf16[192,512]{1,0:T(8,128)(2,1)S(1)}, bf16[192,512]{1,0:T(8,128)(2,1)S(1)}, u32[]{:S(2)}, u32[]{:S(2)}) collective-permute-start(bf16[192,512]{1,0:T(8,128)(2,1)S(1)} %copy-done.2), channel_id=1, source_target_pairs={{0,6},{1,7},{2,4},{3,5},{4,2},{5,3},{6,0},{7,1},{8,14},{9,15},{10,... | collective-permute-start | bytes 589832 | tf_op jit(solution)/shard_map/ppermute | solution.py:268
  16.8 15.4 %collective-permute-start.3 = (bf16[192,512]{1,0:T(8,128)(2,1)S(1)}, bf16[192,512]{1,0:T(8,128)(2,1)S(1)}, u32[]{:S(2)}, u32[]{:S(2)}) collective-permute-start(bf16[192,512]{1,0:T(8,128)(2,1)S(1)} %copy-done.3), channel_id=1, source_target_pairs={{0,6},{1,7},{2,4},{3,5},{4,2},{5,3},{6,0},{7,1},{8,14},{9,15},{10,... | collective-permute-start | bytes 589832 | tf_op jit(solution)/shard_map/ppermute | solution.py:268
  20.4 29.1 %all-to-all-start.1 = ((bf16[16,64,768]{2,1,0:T(8,128)(2,1)}), bf16[16,64,768]{2,1,0:T(8,128)(2,1)S(1)}, u32[]{:S(2)}, u32[]{:S(2)}) async-start(bf16[16,64,768]{2,1,0:T(8,128)(2,1)} %shard_map.77), calls=%async_computation.1 | async-start | bytes 3145728 | tf_op jit(solution)/shard_map/all_to_all | solution.py:255
  24.4 0.7 copy-start.4
  28.1 0.7 copy-start.6
  32.2 0.7 copy-start.8
  32.9 0.9 copy-start.5
  33.8 0.9 copy-start.7
  34.7 0.9 copy-start.9
  112.0 35.3 %all-to-all-start.4 = ((bf16[16,64,576]{2,1,0:T(8,128)(2,1)}), bf16[16,64,576]{2,1,0:T(8,128)(2,1)S(1)}, u32[]{:S(2)}, u32[]{:S(2)}) async-start(bf16[16,64,576]{2,1,0:T(8,128)(2,1)} %get-tuple-element.13), calls=%async_computation.4 | async-start | bytes 2621440 | tf_op jit(solution)/shard_map/all_to_all | solution.py:255
  115.7 31.5 %collective-permute-start.4 = (bf16[576,512]{1,0:T(8,128)(2,1)S(1)}, bf16[576,512]{1,0:T(8,128)(2,1)S(1)}, u32[]{:S(2)}, u32[]{:S(2)}) collective-permute-start(bf16[576,512]{1,0:T(8,128)(2,1)S(1)} %shard_map.80), channel_id=1, source_target_pairs={{0,6},{1,7},{2,4},{3,5},{4,2},{5,3},{6,0},{7,1},{8,14},{9,15},{10,... | collective-permute-start | bytes 1769480 | tf_op jit(solution)/shard_map/ppermute | solution.py:309

commit v3 on v2

--- a/solution.py
+++ b/solution.py
@@ -12,7 +12,9 @@
 AXES = ("phi", "eta")
 LOG2E = 1.4426950408889634
 VMEM_BYTES = 48 * 1024 * 1024
+WHOLE_VMEM_BYTES = 60 * 1024 * 1024
 PACK_FLOPS = 4 * 10**10
+PACK_STEPS = 4
 
 
 def dot(a, b, da, db):
@@ -25,14 +27,12 @@
     return jnp.sum(jnp.where(diagonal, jnp.broadcast_to(row, (count, n)), 0.0), axis=1, keepdims=True)
 
 
-def slots_of(wanted_ref, part, rows, points):
-    group = wanted_ref.shape[0]
-    wanted = wanted_ref[...].astype(jnp.float32)
+def slots_of(wanted_ref, part, rows, points, owners=None):
     places = lax.broadcasted_iota(jnp.int32, (rows, points), 1).astype(jnp.float32)
-    picks = [
-        jnp.where(column_of(wanted[o, :1], part * rows, rows) == places, 1.0, 0.0).astype(jnp.bfloat16)
-        for o in range(group)
-    ]
+    picks = []
+    for o in range(wanted_ref.shape[0]) if owners is None else owners:
+        wanted = wanted_ref[o, :1].astype(jnp.float32)
+        picks.append(jnp.where(column_of(wanted, part * rows, rows) == places, 1.0, 0.0).astype(jnp.bfloat16))
     return jnp.concatenate(picks, axis=0)
 
 
@@ -78,7 +78,7 @@
         wanted_ref[o] = jnp.broadcast_to(wanted[o : o + 1], wanted_ref.shape[1:])
 
 
-def pack_kernel(part, wanted_ref, q_ref, k_ref, v_ref, g_ref, out_ref, features_ref, sems):
+def pack_kernel(part, wanted_ref, q_ref, k_ref, v_ref, g_ref, out_ref, features_ref, packed_ref, sems, out_sems):
     group, rows, width = out_ref.shape
     feat, points = q_ref.shape
     copies = [
@@ -87,11 +87,23 @@
     ]
     for copy in copies:
         copy.start()
-    picks = slots_of(wanted_ref, part, rows, points)
+    share = group // PACK_STEPS
+    picks = [
+        slots_of(wanted_ref, part, rows, points, range(c * share, (c + 1) * share)) for c in range(PACK_STEPS)
+    ]
     for copy in copies:
         copy.wait()
-    packed = dot(picks, features_ref[...], 1, 1)
-    out_ref[...] = packed.astype(jnp.bfloat16).reshape(group, rows, width)
+    features = features_ref[...]
+    results = []
+    for c in range(PACK_STEPS):
+        packed = dot(picks[c], features, 1, 1).astype(jnp.bfloat16)
+        packed_ref[c] = packed.reshape(share, rows, width)
+        results.append(
+            pltpu.make_async_copy(packed_ref.at[c], out_ref.at[pl.ds(c * share, share)], out_sems.at[c])
+        )
+        results[-1].start()
+    for result in results:
+        result.wait()
 
 
 def fold_kernel(wanted_ref, replies_ref, out_ref):
@@ -100,15 +112,14 @@
     out_ref[...] = dot(replies_ref[...].reshape(group * rows, width), picks, 0, 0).astype(jnp.bfloat16)
 
 
-def finish_kernel(wanted_ref, replies_ref, other_ref, q_ref, k_ref, v_ref):
+def keep_kernel(in_ref, out_ref):
+    pass
+
+
+def finish_kernel(wanted_ref, replies_ref, out_ref):
     group, rows, width = replies_ref.shape
-    picks = slots_of(wanted_ref, 0, rows, other_ref.shape[1])
-    total = dot(replies_ref[...].reshape(group * rows, width), picks, 0, 0) + other_ref[...].astype(jnp.float32)
-    total = total.astype(jnp.bfloat16)
-    third = width // 3
-    q_ref[...] = total[:third]
-    k_ref[...] = total[third : 2 * third]
-    v_ref[...] = total[2 * third :]
+    picks = slots_of(wanted_ref, 0, rows, out_ref.shape[1])
+    out_ref[...] = dot(replies_ref[...].reshape(group * rows, width), picks, 0, 0)
 
 
 def attend_kernel(
@@ -218,13 +229,13 @@
             ref[:, low:high, :] = ref[:, low:high, :] + back[part]
 
 
-def call(kernel, out_shape, scratch=(), flops=0, moved=0, in_specs=None):
-    extra = {} if in_specs is None else {"in_specs": in_specs}
+def call(kernel, out_shape, scratch=(), flops=0, moved=0, in_specs=None, out_specs=None, vmem_bytes=VMEM_BYTES):
+    extra = {name: specs for name, specs in (("in_specs", in_specs), ("out_specs", out_specs)) if specs is not None}
     return pl.pallas_call(
         kernel,
         out_shape=out_shape,
         scratch_shapes=list(scratch),
-        compiler_params=pltpu.CompilerParams(vmem_limit_bytes=VMEM_BYTES),
+        compiler_params=pltpu.CompilerParams(vmem_limit_bytes=vmem_bytes),
         cost_estimate=pl.CostEstimate(flops=flops, bytes_accessed=moved, transcendentals=0),
         **extra,
     )
@@ -247,9 +258,8 @@
     bf16 = jnp.bfloat16
     packed = jax.ShapeDtypeStruct((group, rows, 4 * feat), bf16)
     reply = jax.ShapeDtypeStruct((group, rows, 3 * feat), bf16)
-    column = jax.ShapeDtypeStruct((feat, points), bf16)
     steps = points // BUCKET * (HEADS // 2)
-    vmem = pl.BlockSpec(memory_space=pltpu.VMEM)
+    vmem, hbm = pl.BlockSpec(memory_space=pltpu.VMEM), pl.BlockSpec(memory_space=pl.ANY)
 
     def exchange(chunks):
         return lax.all_to_all(chunks, AXES, 0, 0, tiled=True, axis_index_groups=halves)
@@ -258,10 +268,17 @@
         return call(
             functools.partial(pack_kernel, part),
             packed,
-            scratch=(pltpu.VMEM((4 * feat, points), bf16), pltpu.SemaphoreType.DMA((4,))),
+            scratch=(
+                pltpu.VMEM((4 * feat, points), bf16),
+                pltpu.VMEM((PACK_STEPS, group // PACK_STEPS, rows, 4 * feat), bf16),
+                pltpu.SemaphoreType.DMA((4,)),
+                pltpu.SemaphoreType.DMA((PACK_STEPS,)),
+            ),
+            out_specs=pl.BlockSpec(memory_space=pl.ANY),
             in_specs=[vmem] + [pl.BlockSpec(memory_space=pltpu.HBM)] * 4,
             flops=flops,
             moved=2 * group * rows * 4 * feat,
+            vmem_bytes=WHOLE_VMEM_BYTES if part else VMEM_BYTES,
         )
 
     arrays = (query, key_rows, value, out_grad)
@@ -307,14 +324,23 @@
     )
     folded, reply_own = lax.optimization_barrier((fold(wanted, returned_other), reply_own))
     summed = lax.ppermute(folded, AXES, across)
+    summed = pl.pallas_call(
+        keep_kernel,
+        out_shape=jax.ShapeDtypeStruct((3 * feat, points), bf16),
+        in_specs=[hbm],
+        out_specs=hbm,
+        input_output_aliases={0: 0},
+        cost_estimate=pl.CostEstimate(flops=PACK_FLOPS, bytes_accessed=0, transcendentals=0),
+    )(summed)
     returned_own = exchange(reply_own)
     finish = call(
         finish_kernel,
-        (column, column, column),
+        jax.ShapeDtypeStruct((3 * feat, points), jnp.float32),
         flops=2 * group * rows * points * 3 * feat,
         moved=2 * group * rows * 3 * feat,
     )
-    return finish(wanted, returned_own, summed)
+    total = (finish(wanted, returned_own) + summed.astype(jnp.float32)).astype(bf16)
+    return total[:feat], total[feat : 2 * feat], total[2 * feat :]
 
 
 def solution(mesh):

time: 149 us -> 146 us (0.980)
  local copies, waits for them, and re-layouts: 5.5 us -> 3.02 us
    ppermute x1, waiting for transfers between devices: 28.6 us -> 12.2 us  [on_device(): summed = lax.ppermute(folded, AXES, across)]
    all_to_all x3, waiting for transfers between devices: 11.6 us -> 25.9 us  [exchange(): lax.all_to_all(chunks, AXES, 0, 0, tiled=True, axis_index_groups=halves)]
    unnamed x22 -> x26, local copies, waits for them, and re-layouts: 5.5 us -> 2.2 us
    pallas_call x1, Pallas kernels: 2.24 us -> 3.91 us  [on_device(): arrived_other = exchange(pack(1, PACK_FLOPS)(wanted, *copies))]
    ppermute x4, waiting for transfers between devices: 6.46 us -> 8.08 us  [on_device(): copies = [lax.ppermute(array, AXES, across) for array in arrays]]
  transfers between devices with their start and end apart: 8 -> 8, of which waited for: 4 -> 5; matrix products, arithmetic and copies ran while one was open for 0% -> 0% of each run, Pallas kernels for 4% -> 5%
where the time goes in v3:
time: 146 us; the launch traced here: 145 us
  blocking collectives  48.6 us (33%)
  waiting for transfers between devices  46.2 us (32%)
  starting transfers between devices  24.1 us (17%)
  Pallas kernels  22.3 us (15%)
  local copies, waits for them, and re-layouts  3.02 us (2%)
    all_to_all x2, blocking collectives, exchange(): lax.all_to_all(chunks, AXES, 0, 0, tiled=True, axis_index_groups=halves)  48.6 us
    all_to_all x3, waiting for transfers between devices, exchange(): lax.all_to_all(chunks, AXES, 0, 0, tiled=True, axis_index_groups=halves)  25.9 us
    all_to_all x3, starting transfers between devices, exchange(): lax.all_to_all(chunks, AXES, 0, 0, tiled=True, axis_index_groups=halves)  14 us
    ppermute x1, waiting for transfers between devices, on_device(): summed = lax.ppermute(folded, AXES, across)  12.2 us
    pallas_call x1, Pallas kernels, on_device(): reply_own, reply_other = attend(codes, arrived_own, arrived_other)  12.2 us
    ppermute x4, waiting for transfers between devices, on_device(): copies = [lax.ppermute(array, AXES, across) for array in arrays]  8.08 us
    ppermute x4, starting transfers between devices, on_device(): copies = [lax.ppermute(array, AXES, across) for array in arrays]  7.92 us
    pallas_call x1, Pallas kernels, on_device(): arrived_other = exchange(pack(1, PACK_FLOPS)(wanted, *copies))  3.91 us
  transfers between devices with their start and end apart: 8, of which 5 were waited for; matrix products, arithmetic and copies ran while one was open for 0% of the time, Pallas kernels for 5%

profile of v3, /device:TPU:0, one launch (start us, length us, event | category | flops | bytes accessed | tf_op | source)
XLA Modules:
  0.0 145.2 jit_solution(17732747520565108191)
XLA Ops:
  0.6 0.0 copy-start.6
  0.7 0.7 copy-done.6
  1.3 1.3 shard_map.76
  2.7 6.3 %all-to-all-start = ((s32[16,8,128]{2,1,0:T(8,128)}), s32[16,8,128]{2,1,0:T(8,128)S(1)}, u32[]{:S(2)}, u32[]{:S(2)}) async-start(s32[16,8,128]{2,1,0:T(8,128)} %get-tuple-element.9), calls=%async_computation | async-start | bytes 131072 | tf_op jit(solution)/shard_map/all_to_all | solution.py:265
  9.0 4.0 %collective-permute-start = (bf16[192,512]{1,0:T(8,128)(2,1)S(1)}, bf16[192,512]{1,0:T(8,128)(2,1)S(1)}, u32[]{:S(2)}, u32[]{:S(2)}) collective-permute-start(bf16[192,512]{1,0:T(8,128)(2,1)S(1)} %copy-done.2), channel_id=1, source_target_pairs={{0,6},{1,7},{2,4},{3,5},{4,2},{5,3},{6,0},{7,1},{8,14},{9,15},{10,... | collective-permute-start | bytes 589832 | tf_op jit(solution)/shard_map/ppermute | solution.py:285
  13.0 0.1 collective-permute-start.1
  13.1 3.7 %collective-permute-start.2 = (bf16[192,512]{1,0:T(8,128)(2,1)S(1)}, bf16[192,512]{1,0:T(8,128)(2,1)S(1)}, u32[]{:S(2)}, u32[]{:S(2)}) collective-permute-start(bf16[192,512]{1,0:T(8,128)(2,1)S(1)} %copy-done.4), channel_id=1, source_target_pairs={{0,6},{1,7},{2,4},{3,5},{4,2},{5,3},{6,0},{7,1},{8,14},{9,15},{10,... | collective-permute-start | bytes 589832 | tf_op jit(solution)/shard_map/ppermute | solution.py:285
  16.8 0.1 collective-permute-start.3
  16.9 0.0 all-to-all-done.wanted_ref
  16.9 3.1 %shard_map.77 = bf16[16,64,768]{2,1,0:T(8,128)(2,1)} custom-call(s32[16,8,128]{2,1,0:T(8,128)S(1)} %all-to-all-done.wanted_ref, bf16[192,512]{1,0:T(8,128)(2,1)S(1)} %copy-done.2, bf16[192,512]{1,0:T(8,128)(2,1)S(1)} %copy-done.3, bf16[192,512]{1,0:T(8,128)(2,1)S(1)} %copy-done.4, bf16[192,512]{1,0:T(8,128)(2,1)S(1)} %copy-done.5), custom_call_target="tpu_custom_call" | custom-call | flops 805306368 | bytes 1572864 | tf_op jit(solution)/shard_map/pallas_call | solution.py:300
  20.1 4.0 %all-to-all-start.1 = ((bf16[16,64,768]{2,1,0:T(8,128)(2,1)}), bf16[16,64,768]{2,1,0:T(8,128)(2,1)S(1)}, u32[]{:S(2)}, u32[]{:S(2)}) async-start(bf16[16,64,768]{2,1,0:T(8,128)(2,1)} %shard_map.77), calls=%async_computation.1 | async-start | bytes 3145728 | tf_op jit(solution)/shard_map/all_to_all | solution.py:265
  24.1 0.0 collective-permute-done.q_ref
  24.1 0.0 copy-start.9
  24.1 0.0 collective-permute-done.1.k_ref
  24.1 0.0 copy-start.10
  24.1 4.0 %collective-permute-done.2.v_ref = bf16[192,512]{1,0:T(8,128)(2,1)S(1)} collective-permute-done((bf16[192,512]{1,0:T(8,128)(2,1)S(1)}, bf16[192,512]{1,0:T(8,128)(2,1)S(1)}, u32[]{:S(2)}, u32[]{:S(2)}) %collective-permute-start.2) | collective-permute-done | bytes 196640 | tf_op jit(solution)/shard_map/ppermute | solution.py:285
  28.1 4.1 %collective-permute-done.3.g_ref = bf16[192,512]{1,0:T(8,128)(2,1)S(1)} collective-permute-done((bf16[192,512]{1,0:T(8,128)(2,1)S(1)}, bf16[192,512]{1,0:T(8,128)(2,1)S(1)}, u32[]{:S(2)}, u32[]{:S(2)}) %collective-permute-start.3) | collective-permute-done | bytes 196640 | tf_op jit(solution)/shard_map/ppermute | solution.py:285
  32.2 0.7 copy-done.12
  32.9 3.9 %shard_map.78 = bf16[16,64,768]{2,1,0:T(8,128)(2,1)} custom-call(s32[16,8,128]{2,1,0:T(8,128)} %copy-done, bf16[192,512]{1,0:T(8,128)(2,1)} %copy-done.9, bf16[192,512]{1,0:T(8,128)(2,1)} %copy-done.10, bf16[192,512]{1,0:T(8,128)(2,1)} %copy-done.11, bf16[192,512]{1,0:T(8,128)(2,1)} %copy-done.12), custom_call_target="tpu_custom_call" | custom-call | flops 40000000000 | bytes 1572864 | tf_op jit(solution)/shard_map/pallas_call | solution.py:301
  36.8 12.7 %all-to-all-done.1.own_ref = bf16[16,64,768]{2,1,0:T(8,128)(2,1)S(1)} async-done(((bf16[16,64,768]{2,1,0:T(8,128)(2,1)}), bf16[16,64,768]{2,1,0:T(8,128)(2,1)S(1)}, u32[]{:S(2)}, u32[]{:S(2)}) %all-to-all-start.1) | async-done | bytes 1572896 | tf_op jit(solution)/shard_map/all_to_all | solution.py:265
  49.5 27.4 %all_to_all.25.other_ref = bf16[16,64,768]{2,1,0:T(8,128)(2,1)S(1)} all-to-all(bf16[16,64,768]{2,1,0:T(8,128)(2,1)} %shard_map.78), channel_id=1, replica_groups={{0,1,2,3,8,9,10,11,16,17,18,19,24,25,26,27},{4,5,6,7,12,13,14,15,20,21,..., dimensions={0} | all-to-all | bytes 3145728 | tf_op jit(solution)/shard_map/all_to_all | solution.py:265
  76.9 12.2 %shard_map.79 = (bf16[16,64,576]{2,1,0:T(8,128)(2,1)}, bf16[16,64,576]{2,1,0:T(8,128)(2,1)S(1)}) custom-call(s32[3,512]{1,0:T(4,128)S(1)} %get-tuple-element.10.codes_ref, bf16[16,64,768]{2,1,0:T(8,128)(2,1)S(1)} %all-to-all-done.1.own_ref, bf16[16,64,768]{2,1,0:T(8,128)(2,1)S(1)} %all_to_all.25.other_ref), custom_call_target="tpu_custom_call" | custom-call | flops 20000000000 | bytes 8000000 | tf_op jit(solution)/shard_map/pallas_call | solution.py:317
  89.1 21.2 %all_to_all.26.replies_ref = bf16[16,64,576]{2,1,0:T(8,128)(2,1)S(1)} all-to-all(bf16[16,64,576]{2,1,0:T(8,128)(2,1)S(1)} %get-tuple-element.11), channel_id=1, replica_groups={{0,1,2,3,8,9,10,11,16,17,18,19,24,25,26,27},{4,5,6,7,12,13,14,15,20,21,..., dimensions={0} | all-to-all | bytes 2359296 | tf_op jit(solution)/shard_map/all_to_all | solution.py:265
  110.3 0.9 shard_map.80
  111.2 2.2 %collective-permute-start.4 = (bf16[576,512]{1,0:T(8,128)(2,1)S(1)}, bf16[576,512]{1,0:T(8,128)(2,1)S(1)}, u32[]{:S(2)}, u32[]{:S(2)}) collective-permute-start(bf16[576,512]{1,0:T(8,128)(2,1)S(1)} %shard_map.80), channel_id=1, source_target_pairs={{0,6},{1,7},{2,4},{3,5},{4,2},{5,3},{6,0},{7,1},{8,14},{9,15},{10,... | collective-permute-start | bytes 1769480 | tf_op jit(solution)/shard_map/ppermute | solution.py:326
  113.4 3.7 %all-to-all-start.4 = ((bf16[16,64,576]{2,1,0:T(8,128)(2,1)}), bf16[16,64,576]{2,1,0:T(8,128)(2,1)S(1)}, u32[]{:S(2)}, u32[]{:S(2)}) async-start(bf16[16,64,576]{2,1,0:T(8,128)(2,1)} %get-tuple-element.13), calls=%async_computation.4 | async-start | bytes 2621440 | tf_op jit(solution)/shard_map/all_to_all | solution.py:265
  117.1 12.2 %collective-permute-done.4.in_ref = bf16[576,512]{1,0:T(8,128)(2,1)S(1)} collective-permute-done((bf16[576,512]{1,0:T(8,128)(2,1)S(1)}, bf16[576,512]{1,0:T(8,128)(2,1)S(1)}, u32[]{:S(2)}, u32[]{:S(2)}) %collective-permute-start.4) | collective-permute-done | bytes 589856 | tf_op jit(solution)/shard_map/ppermute | solution.py:326
  129.3 0.8 copy-done.7
  130.1 13.2 %all-to-all-done.4.replies_ref = bf16[16,64,576]{2,1,0:T(8,128)(2,1)S(1)} async-done(((bf16[16,64,576]{2,1,0:T(8,128)(2,1)}), bf16[16,64,576]{2,1,0:T(8,128)(2,1)S(1)}, u32[]{:S(2)}, u32[]{:S(2)}) %all-to-all-start.4) | async-done | bytes 1179680 | tf_op jit(solution)/shard_map/all_to_all | solution.py:265
  143.3 0.9 shard_map.81
  144.2 0.2 add_convert_fusion
  144.4 0.8 fusion
  (21 shorter events, 0.0 us)
Async XLA Ops:
  0.6 0.7 copy-start.6
  1.3 7.7 %copy-start.2 = (bf16[192,512]{1,0:T(8,128)(2,1)S(1)}, bf16[192,512]{1,0:T(8,128)(2,1)}, u32[]{:S(2)}) copy-start(bf16[192,512]{1,0:T(8,128)(2,1)} %q_ref.1) | copy-start | bytes 589828
  1.3 11.7 %copy-start.3 = (bf16[192,512]{1,0:T(8,128)(2,1)S(1)}, bf16[192,512]{1,0:T(8,128)(2,1)}, u32[]{:S(2)}) copy-start(bf16[192,512]{1,0:T(8,128)(2,1)} %k_ref.1) | copy-start | bytes 589828
  1.3 11.8 %copy-start.4 = (bf16[192,512]{1,0:T(8,128)(2,1)S(1)}, bf16[192,512]{1,0:T(8,128)(2,1)}, u32[]{:S(2)}) copy-start(bf16[192,512]{1,0:T(8,128)(2,1)} %v_ref.1) | copy-start | bytes 589828
  1.3 15.5 %copy-start.5 = (bf16[192,512]{1,0:T(8,128)(2,1)S(1)}, bf16[192,512]{1,0:T(8,128)(2,1)}, u32[]{:S(2)}) copy-start(bf16[192,512]{1,0:T(8,128)(2,1)} %g_ref.1) | copy-start | bytes 589828
  2.7 14.2 %all-to-all-start = ((s32[16,8,128]{2,1,0:T(8,128)}), s32[16,8,128]{2,1,0:T(8,128)S(1)}, u32[]{:S(2)}, u32[]{:S(2)}) async-start(s32[16,8,128]{2,1,0:T(8,128)} %get-tuple-element.9), calls=%async_computation | async-start | bytes 131072 | tf_op jit(solution)/shard_map/all_to_all | solution.py:265
  9.0 15.1 %collective-permute-start = (bf16[192,512]{1,0:T(8,128)(2,1)S(1)}, bf16[192,512]{1,0:T(8,128)(2,1)S(1)}, u32[]{:S(2)}, u32[]{:S(2)}) collective-permute-start(bf16[192,512]{1,0:T(8,128)(2,1)S(1)} %copy-done.2), channel_id=1, source_target_pairs={{0,6},{1,7},{2,4},{3,5},{4,2},{5,3},{6,0},{7,1},{8,14},{9,15},{10,... | collective-permute-start | bytes 589832 | tf_op jit(solution)/shard_map/ppermute | solution.py:285
  13.0 11.1 %collective-permute-start.1 = (bf16[192,512]{1,0:T(8,128)(2,1)S(1)}, bf16[192,512]{1,0:T(8,128)(2,1)S(1)}, u32[]{:S(2)}, u32[]{:S(2)}) collective-permute-start(bf16[192,512]{1,0:T(8,128)(2,1)S(1)} %copy-done.3), channel_id=1, source_target_pairs={{0,6},{1,7},{2,4},{3,5},{4,2},{5,3},{6,0},{7,1},{8,14},{9,15},{10,... | collective-permute-start | bytes 589832 | tf_op jit(solution)/shard_map/ppermute | solution.py:285
  13.1 15.0 %collective-permute-start.2 = (bf16[192,512]{1,0:T(8,128)(2,1)S(1)}, bf16[192,512]{1,0:T(8,128)(2,1)S(1)}, u32[]{:S(2)}, u32[]{:S(2)}) collective-permute-start(bf16[192,512]{1,0:T(8,128)(2,1)S(1)} %copy-done.4), channel_id=1, source_target_pairs={{0,6},{1,7},{2,4},{3,5},{4,2},{5,3},{6,0},{7,1},{8,14},{9,15},{10,... | collective-permute-start | bytes 589832 | tf_op jit(solution)/shard_map/ppermute | solution.py:285
  16.8 15.4 %collective-permute-start.3 = (bf16[192,512]{1,0:T(8,128)(2,1)S(1)}, bf16[192,512]{1,0:T(8,128)(2,1)S(1)}, u32[]{:S(2)}, u32[]{:S(2)}) collective-permute-start(bf16[192,512]{1,0:T(8,128)(2,1)S(1)} %copy-done.5), channel_id=1, source_target_pairs={{0,6},{1,7},{2,4},{3,5},{4,2},{5,3},{6,0},{7,1},{8,14},{9,15},{10,... | collective-permute-start | bytes 589832 | tf_op jit(solution)/shard_map/ppermute | solution.py:285
  16.9 3.1 %copy-start = (s32[16,8,128]{2,1,0:T(8,128)}, s32[16,8,128]{2,1,0:T(8,128)S(1)}, u32[]{:S(2)}) copy-start(s32[16,8,128]{2,1,0:T(8,128)S(1)} %all-to-all-done.wanted_ref) | copy-start | bytes 196612
  20.1 29.4 %all-to-all-start.1 = ((bf16[16,64,768]{2,1,0:T(8,128)(2,1)}), bf16[16,64,768]{2,1,0:T(8,128)(2,1)S(1)}, u32[]{:S(2)}, u32[]{:S(2)}) async-start(bf16[16,64,768]{2,1,0:T(8,128)(2,1)} %shard_map.77), calls=%async_computation.1 | async-start | bytes 3145728 | tf_op jit(solution)/shard_map/all_to_all | solution.py:265
  24.1 8.1 %copy-start.9 = (bf16[192,512]{1,0:T(8,128)(2,1)}, bf16[192,512]{1,0:T(8,128)(2,1)S(1)}, u32[]{:S(2)}) copy-start(bf16[192,512]{1,0:T(8,128)(2,1)S(1)} %collective-permute-done.q_ref) | copy-start | bytes 589828
  24.1 8.1 %copy-start.10 = (bf16[192,512]{1,0:T(8,128)(2,1)}, bf16[192,512]{1,0:T(8,128)(2,1)S(1)}, u32[]{:S(2)}) copy-start(bf16[192,512]{1,0:T(8,128)(2,1)S(1)} %collective-permute-done.1.k_ref) | copy-start | bytes 589828
  28.1 4.1 %copy-start.11 = (bf16[192,512]{1,0:T(8,128)(2,1)}, bf16[192,512]{1,0:T(8,128)(2,1)S(1)}, u32[]{:S(2)}) copy-start(bf16[192,512]{1,0:T(8,128)(2,1)S(1)} %collective-permute-done.2.v_ref) | copy-start | bytes 589828
  32.2 0.7 copy-start.12
  89.1 21.2 %copy-start.1 = (s32[16,8,128]{2,1,0:T(8,128)S(1)}, s32[16,8,128]{2,1,0:T(8,128)}, u32[]{:S(2)}) copy-start(s32[16,8,128]{2,1,0:T(8,128)} %copy-done) | copy-start | bytes 196612
  111.2 18.1 %collective-permute-start.4 = (bf16[576,512]{1,0:T(8,128)(2,1)S(1)}, bf16[576,512]{1,0:T(8,128)(2,1)S(1)}, u32[]{:S(2)}, u32[]{:S(2)}) collective-permute-start(bf16[576,512]{1,0:T(8,128)(2,1)S(1)} %shard_map.80), channel_id=1, source_target_pairs={{0,6},{1,7},{2,4},{3,5},{4,2},{5,3},{6,0},{7,1},{8,14},{9,15},{10,... | collective-permute-start | bytes 1769480 | tf_op jit(solution)/shard_map/ppermute | solution.py:326
  113.4 29.9 %all-to-all-start.4 = ((bf16[16,64,576]{2,1,0:T(8,128)(2,1)}), bf16[16,64,576]{2,1,0:T(8,128)(2,1)S(1)}, u32[]{:S(2)}, u32[]{:S(2)}) async-start(bf16[16,64,576]{2,1,0:T(8,128)(2,1)} %get-tuple-element.13), calls=%async_computation.4 | async-start | bytes 2621440 | tf_op jit(solution)/shard_map/all_to_all | solution.py:265
  129.3 0.8 copy-start.7
  130.1 14.1 %copy-start.8 = (bf16[576,512]{1,0:T(8,128)(2,1)S(1)}, bf16[576,512]{1,0:T(8,128)(2,1)}, u32[]{:S(2)}) copy-start(bf16[576,512]{1,0:T(8,128)(2,1)} %shard_map.82) | copy-start | bytes 1769476

commit v4 on v3

--- a/solution.py
+++ b/solution.py
@@ -12,7 +12,7 @@
 AXES = ("phi", "eta")
 LOG2E = 1.4426950408889634
 VMEM_BYTES = 48 * 1024 * 1024
-WHOLE_VMEM_BYTES = 60 * 1024 * 1024
+WHOLE_VMEM_BYTES = 62 * 1024 * 1024
 PACK_FLOPS = 4 * 10**10
 PACK_STEPS = 4
 
@@ -116,10 +116,13 @@
     pass
 
 
-def finish_kernel(wanted_ref, replies_ref, out_ref):
+def finish_kernel(wanted_ref, replies_ref, q_ref, k_ref, v_ref):
     group, rows, width = replies_ref.shape
-    picks = slots_of(wanted_ref, 0, rows, out_ref.shape[1])
-    out_ref[...] = dot(replies_ref[...].reshape(group * rows, width), picks, 0, 0)
+    feat, points = q_ref.shape
+    picks = slots_of(wanted_ref, 0, rows, points)
+    total = dot(replies_ref[...].reshape(group * rows, width), picks, 0, 0)
+    for n, ref in enumerate((q_ref, k_ref, v_ref)):
+        ref[...] = total[n * feat : (n + 1) * feat]
 
 
 def attend_kernel(
@@ -278,7 +281,7 @@
             in_specs=[vmem] + [pl.BlockSpec(memory_space=pltpu.HBM)] * 4,
             flops=flops,
             moved=2 * group * rows * 4 * feat,
-            vmem_bytes=WHOLE_VMEM_BYTES if part else VMEM_BYTES,
+            vmem_bytes=WHOLE_VMEM_BYTES,
         )
 
     arrays = (query, key_rows, value, out_grad)
@@ -335,12 +338,14 @@
     returned_own = exchange(reply_own)
     finish = call(
         finish_kernel,
-        jax.ShapeDtypeStruct((3 * feat, points), jnp.float32),
+        (jax.ShapeDtypeStruct((feat, points), jnp.float32),) * 3,
         flops=2 * group * rows * points * 3 * feat,
         moved=2 * group * rows * 3 * feat,
     )
-    total = (finish(wanted, returned_own) + summed.astype(jnp.float32)).astype(bf16)
-    return total[:feat], total[feat : 2 * feat], total[2 * feat :]
+    own_sums = finish(wanted, returned_own)
+    return tuple(
+        (own + summed[n * feat : (n + 1) * feat].astype(jnp.float32)).astype(bf16) for n, own in enumerate(own_sums)
+    )
 
 
 def solution(mesh):

time: 146 us -> 145 us (level)
  blocking collectives: 48.6 us -> 47.1 us
    all_to_all x3, waiting for transfers between devices: 25.9 us -> 27.8 us  [exchange(): lax.all_to_all(chunks, AXES, 0, 0, tiled=True, axis_index_groups=halves)]
    ppermute x4, waiting for transfers between devices: 8.08 us -> 6.42 us  [on_device(): copies = [lax.ppermute(array, AXES, across) for array in arrays]]
    all_to_all x2, blocking collectives: 48.6 us -> 47.1 us  [exchange(): lax.all_to_all(chunks, AXES, 0, 0, tiled=True, axis_index_groups=halves)]
where the time goes in v4:
time: 145 us
  blocking collectives  47.1 us (32%)
  waiting for transfers between devices  46.4 us (32%)
  starting transfers between devices  24.1 us (17%)
  Pallas kernels  23.1 us (16%)
  local copies, waits for them, and re-layouts  2.14 us (1%)
    all_to_all x2, blocking collectives, exchange(): lax.all_to_all(chunks, AXES, 0, 0, tiled=True, axis_index_groups=halves)  47.1 us
    all_to_all x3, waiting for transfers between devices, exchange(): lax.all_to_all(chunks, AXES, 0, 0, tiled=True, axis_index_groups=halves)  27.8 us
    all_to_all x3, starting transfers between devices, exchange(): lax.all_to_all(chunks, AXES, 0, 0, tiled=True, axis_index_groups=halves)  14 us
    pallas_call x1, Pallas kernels, on_device(): reply_own, reply_other = attend(codes, arrived_own, arrived_other)  12.2 us
    ppermute x1, waiting for transfers between devices, on_device(): summed = lax.ppermute(folded, AXES, across)  12.2 us
    ppermute x4, starting transfers between devices, on_device(): copies = [lax.ppermute(array, AXES, across) for array in arrays]  7.92 us
    ppermute x4, waiting for transfers between devices, on_device(): copies = [lax.ppermute(array, AXES, across) for array in arrays]  6.42 us
    pallas_call x1, Pallas kernels, on_device(): pack(0, 2 * group * rows * points * 4 * feat)(wanted, *arrays)  3.94 us
  transfers between devices with their start and end apart: 8, of which 5 were waited for; matrix products, arithmetic and copies ran while one was open for 0% of the time, Pallas kernels for 5%

profile of v4, /device:TPU:0, one launch (start us, length us, event | category | flops | bytes accessed | tf_op | source)
XLA Modules:
  0.0 144.5 jit_solution(14809483062653539344)
XLA Ops:
  0.6 0.0 copy-start.2
  0.7 0.7 copy-done.2
  1.3 1.3 shard_map.76
  2.7 6.3 %all-to-all-start = ((s32[16,8,128]{2,1,0:T(8,128)}), s32[16,8,128]{2,1,0:T(8,128)S(1)}, u32[]{:S(2)}, u32[]{:S(2)}) async-start(s32[16,8,128]{2,1,0:T(8,128)} %get-tuple-element.12), calls=%async_computation | async-start | bytes 131072 | tf_op jit(solution)/shard_map/all_to_all | solution.py:268
  9.0 0.0 copy-done.5
  9.0 4.0 %collective-permute-start = (bf16[192,512]{1,0:T(8,128)(2,1)S(1)}, bf16[192,512]{1,0:T(8,128)(2,1)}, u32[]{:S(2)}, u32[]{:S(2)}) collective-permute-start(bf16[192,512]{1,0:T(8,128)(2,1)S(1)} %copy-done.5), channel_id=1, source_target_pairs={{0,6},{1,7},{2,4},{3,5},{4,2},{5,3},{6,0},{7,1},{8,14},{9,15},{10,... | collective-permute-start | bytes 589832 | tf_op jit(solution)/shard_map/ppermute | solution.py:288
  13.0 0.0 copy-done.6
  13.0 0.1 collective-permute-start.1
  13.1 3.7 %collective-permute-start.2 = (bf16[192,512]{1,0:T(8,128)(2,1)}, bf16[192,512]{1,0:T(8,128)(2,1)}, u32[]{:S(2)}, u32[]{:S(2)}) collective-permute-start(bf16[192,512]{1,0:T(8,128)(2,1)} %v_ref.1), channel_id=1, source_target_pairs={{0,6},{1,7},{2,4},{3,5},{4,2},{5,3},{6,0},{7,1},{8,14},{9,15},{10,... | collective-permute-start | bytes 589832 | tf_op jit(solution)/shard_map/ppermute | solution.py:288
  16.8 0.1 collective-permute-start.3
  16.9 0.0 all-to-all-done.wanted_ref
  16.9 0.6 copy-done
  17.6 3.9 %shard_map.77 = bf16[16,64,768]{2,1,0:T(8,128)(2,1)} custom-call(s32[16,8,128]{2,1,0:T(8,128)} %copy-done, bf16[192,512]{1,0:T(8,128)(2,1)} %q_ref.1, bf16[192,512]{1,0:T(8,128)(2,1)} %k_ref.1, bf16[192,512]{1,0:T(8,128)(2,1)} %v_ref.1, bf16[192,512]{1,0:T(8,128)(2,1)} %g_ref.1), custom_call_target="tpu_custom_call" | custom-call | flops 805306368 | bytes 1572864 | tf_op jit(solution)/shard_map/pallas_call | solution.py:303
  21.5 4.0 %all-to-all-start.1 = ((bf16[16,64,768]{2,1,0:T(8,128)(2,1)}), bf16[16,64,768]{2,1,0:T(8,128)(2,1)S(1)}, u32[]{:S(2)}, u32[]{:S(2)}) async-start(bf16[16,64,768]{2,1,0:T(8,128)(2,1)} %shard_map.77), calls=%async_computation.1 | async-start | bytes 3145728 | tf_op jit(solution)/shard_map/all_to_all | solution.py:268
  25.5 0.0 collective-permute-done.q_ref
  25.5 0.0 collective-permute-done.1.k_ref
  25.5 2.6 %collective-permute-done.2.v_ref = bf16[192,512]{1,0:T(8,128)(2,1)} collective-permute-done((bf16[192,512]{1,0:T(8,128)(2,1)}, bf16[192,512]{1,0:T(8,128)(2,1)}, u32[]{:S(2)}, u32[]{:S(2)}) %collective-permute-start.2) | collective-permute-done | bytes 196640 | tf_op jit(solution)/shard_map/ppermute | solution.py:288
  28.1 3.8 %collective-permute-done.3.g_ref = bf16[192,512]{1,0:T(8,128)(2,1)} collective-permute-done((bf16[192,512]{1,0:T(8,128)(2,1)}, bf16[192,512]{1,0:T(8,128)(2,1)}, u32[]{:S(2)}, u32[]{:S(2)}) %collective-permute-start.3) | collective-permute-done | bytes 196640 | tf_op jit(solution)/shard_map/ppermute | solution.py:288
  31.9 3.9 %shard_map.78 = bf16[16,64,768]{2,1,0:T(8,128)(2,1)} custom-call(s32[16,8,128]{2,1,0:T(8,128)} %copy-done, bf16[192,512]{1,0:T(8,128)(2,1)} %collective-permute-done.q_ref, bf16[192,512]{1,0:T(8,128)(2,1)} %collective-permute-done.1.k_ref, bf16[192,512]{1,0:T(8,128)(2,1)} %collective-permute-done.2.v_ref, bf16[192,512]{1,0:T(8,128)(2,1)} %collective-permute-done.3.g_ref), custom_call_target="tpu_custom_call" | custom-call | flops 40000000000 | bytes 1572864 | tf_op jit(solution)/shard_map/pallas_call | solution.py:304
  35.9 14.6 %all-to-all-done.1.own_ref = bf16[16,64,768]{2,1,0:T(8,128)(2,1)S(1)} async-done(((bf16[16,64,768]{2,1,0:T(8,128)(2,1)}), bf16[16,64,768]{2,1,0:T(8,128)(2,1)S(1)}, u32[]{:S(2)}, u32[]{:S(2)}) %all-to-all-start.1) | async-done | bytes 1572896 | tf_op jit(solution)/shard_map/all_to_all | solution.py:268
  50.4 25.9 %all_to_all.25.other_ref = bf16[16,64,768]{2,1,0:T(8,128)(2,1)S(1)} all-to-all(bf16[16,64,768]{2,1,0:T(8,128)(2,1)} %shard_map.78), channel_id=1, replica_groups={{0,1,2,3,8,9,10,11,16,17,18,19,24,25,26,27},{4,5,6,7,12,13,14,15,20,21,..., dimensions={0} | all-to-all | bytes 3145728 | tf_op jit(solution)/shard_map/all_to_all | solution.py:268
  76.4 12.2 %shard_map.79 = (bf16[16,64,576]{2,1,0:T(8,128)(2,1)}, bf16[16,64,576]{2,1,0:T(8,128)(2,1)S(1)}) custom-call(s32[3,512]{1,0:T(4,128)S(1)} %get-tuple-element.13.codes_ref, bf16[16,64,768]{2,1,0:T(8,128)(2,1)S(1)} %all-to-all-done.1.own_ref, bf16[16,64,768]{2,1,0:T(8,128)(2,1)S(1)} %all_to_all.25.other_ref), custom_call_target="tpu_custom_call" | custom-call | flops 20000000000 | bytes 8000000 | tf_op jit(solution)/shard_map/pallas_call | solution.py:320
  88.6 21.2 %all_to_all.26.replies_ref = bf16[16,64,576]{2,1,0:T(8,128)(2,1)S(1)} all-to-all(bf16[16,64,576]{2,1,0:T(8,128)(2,1)S(1)} %get-tuple-element.14), channel_id=1, replica_groups={{0,1,2,3,8,9,10,11,16,17,18,19,24,25,26,27},{4,5,6,7,12,13,14,15,20,21,..., dimensions={0} | all-to-all | bytes 2359296 | tf_op jit(solution)/shard_map/all_to_all | solution.py:268
  109.8 0.0 copy-done.1
  109.8 0.9 shard_map.80
  110.6 2.2 %collective-permute-start.4 = (bf16[576,512]{1,0:T(8,128)(2,1)S(1)}, bf16[576,512]{1,0:T(8,128)(2,1)S(1)}, u32[]{:S(2)}, u32[]{:S(2)}) collective-permute-start(bf16[576,512]{1,0:T(8,128)(2,1)S(1)} %shard_map.80), channel_id=1, source_target_pairs={{0,6},{1,7},{2,4},{3,5},{4,2},{5,3},{6,0},{7,1},{8,14},{9,15},{10,... | collective-permute-start | bytes 1769480 | tf_op jit(solution)/shard_map/ppermute | solution.py:329
  112.8 3.7 %all-to-all-start.4 = ((bf16[16,64,576]{2,1,0:T(8,128)(2,1)}), bf16[16,64,576]{2,1,0:T(8,128)(2,1)S(1)}, u32[]{:S(2)}, u32[]{:S(2)}) async-start(bf16[16,64,576]{2,1,0:T(8,128)(2,1)} %get-tuple-element.16), calls=%async_computation.4 | async-start | bytes 2621440 | tf_op jit(solution)/shard_map/all_to_all | solution.py:268
  116.6 12.2 %collective-permute-done.4.in_ref = bf16[576,512]{1,0:T(8,128)(2,1)S(1)} collective-permute-done((bf16[576,512]{1,0:T(8,128)(2,1)S(1)}, bf16[576,512]{1,0:T(8,128)(2,1)S(1)}, u32[]{:S(2)}, u32[]{:S(2)}) %collective-permute-start.4) | collective-permute-done | bytes 589856 | tf_op jit(solution)/shard_map/ppermute | solution.py:329
  128.7 0.8 copy-done.3
  129.6 13.2 %all-to-all-done.4.replies_ref = bf16[16,64,576]{2,1,0:T(8,128)(2,1)S(1)} async-done(((bf16[16,64,576]{2,1,0:T(8,128)(2,1)}), bf16[16,64,576]{2,1,0:T(8,128)(2,1)S(1)}, u32[]{:S(2)}, u32[]{:S(2)}) %all-to-all-start.4) | async-done | bytes 1179680 | tf_op jit(solution)/shard_map/all_to_all | solution.py:268
  142.8 0.9 shard_map.81
  143.6 0.9 add_convert_fusion
  (8 shorter events, 0.0 us)
Async XLA Ops:
  0.6 0.7 copy-start.2
  1.3 7.6 %copy-start.5 = (bf16[192,512]{1,0:T(8,128)(2,1)S(1)}, bf16[192,512]{1,0:T(8,128)(2,1)}, u32[]{:S(2)}) copy-start(bf16[192,512]{1,0:T(8,128)(2,1)} %q_ref.1) | copy-start | bytes 589828
  1.3 11.7 %copy-start.6 = (bf16[192,512]{1,0:T(8,128)(2,1)S(1)}, bf16[192,512]{1,0:T(8,128)(2,1)}, u32[]{:S(2)}) copy-start(bf16[192,512]{1,0:T(8,128)(2,1)} %k_ref.1) | copy-start | bytes 589828
  2.7 14.2 %all-to-all-start = ((s32[16,8,128]{2,1,0:T(8,128)}), s32[16,8,128]{2,1,0:T(8,128)S(1)}, u32[]{:S(2)}, u32[]{:S(2)}) async-start(s32[16,8,128]{2,1,0:T(8,128)} %get-tuple-element.12), calls=%async_computation | async-start | bytes 131072 | tf_op jit(solution)/shard_map/all_to_all | solution.py:268
  9.0 16.5 %collective-permute-start = (bf16[192,512]{1,0:T(8,128)(2,1)S(1)}, bf16[192,512]{1,0:T(8,128)(2,1)}, u32[]{:S(2)}, u32[]{:S(2)}) collective-permute-start(bf16[192,512]{1,0:T(8,128)(2,1)S(1)} %copy-done.5), channel_id=1, source_target_pairs={{0,6},{1,7},{2,4},{3,5},{4,2},{5,3},{6,0},{7,1},{8,14},{9,15},{10,... | collective-permute-start | bytes 589832 | tf_op jit(solution)/shard_map/ppermute | solution.py:288
  13.0 12.5 %collective-permute-start.1 = (bf16[192,512]{1,0:T(8,128)(2,1)S(1)}, bf16[192,512]{1,0:T(8,128)(2,1)}, u32[]{:S(2)}, u32[]{:S(2)}) collective-permute-start(bf16[192,512]{1,0:T(8,128)(2,1)S(1)} %copy-done.6), channel_id=1, source_target_pairs={{0,6},{1,7},{2,4},{3,5},{4,2},{5,3},{6,0},{7,1},{8,14},{9,15},{10,... | collective-permute-start | bytes 589832 | tf_op jit(solution)/shard_map/ppermute | solution.py:288
  13.1 15.0 %collective-permute-start.2 = (bf16[192,512]{1,0:T(8,128)(2,1)}, bf16[192,512]{1,0:T(8,128)(2,1)}, u32[]{:S(2)}, u32[]{:S(2)}) collective-permute-start(bf16[192,512]{1,0:T(8,128)(2,1)} %v_ref.1), channel_id=1, source_target_pairs={{0,6},{1,7},{2,4},{3,5},{4,2},{5,3},{6,0},{7,1},{8,14},{9,15},{10,... | collective-permute-start | bytes 589832 | tf_op jit(solution)/shard_map/ppermute | solution.py:288
  16.8 15.1 %collective-permute-start.3 = (bf16[192,512]{1,0:T(8,128)(2,1)}, bf16[192,512]{1,0:T(8,128)(2,1)}, u32[]{:S(2)}, u32[]{:S(2)}) collective-permute-start(bf16[192,512]{1,0:T(8,128)(2,1)} %g_ref.1), channel_id=1, source_target_pairs={{0,6},{1,7},{2,4},{3,5},{4,2},{5,3},{6,0},{7,1},{8,14},{9,15},{10,... | collective-permute-start | bytes 589832 | tf_op jit(solution)/shard_map/ppermute | solution.py:288
  16.9 0.6 copy-start
  21.5 29.0 %all-to-all-start.1 = ((bf16[16,64,768]{2,1,0:T(8,128)(2,1)}), bf16[16,64,768]{2,1,0:T(8,128)(2,1)S(1)}, u32[]{:S(2)}, u32[]{:S(2)}) async-start(bf16[16,64,768]{2,1,0:T(8,128)(2,1)} %shard_map.77), calls=%async_computation.1 | async-start | bytes 3145728 | tf_op jit(solution)/shard_map/all_to_all | solution.py:268
  88.5 21.2 %copy-start.1 = (s32[16,8,128]{2,1,0:T(8,128)S(1)}, s32[16,8,128]{2,1,0:T(8,128)}, u32[]{:S(2)}) copy-start(s32[16,8,128]{2,1,0:T(8,128)} %copy-done) | copy-start | bytes 196612
  110.6 18.1 %collective-permute-start.4 = (bf16[576,512]{1,0:T(8,128)(2,1)S(1)}, bf16[576,512]{1,0:T(8,128)(2,1)S(1)}, u32[]{:S(2)}, u32[]{:S(2)}) collective-permute-start(bf16[576,512]{1,0:T(8,128)(2,1)S(1)} %shard_map.80), channel_id=1, source_target_pairs={{0,6},{1,7},{2,4},{3,5},{4,2},{5,3},{6,0},{7,1},{8,14},{9,15},{10,... | collective-permute-start | bytes 1769480 | tf_op jit(solution)/shard_map/ppermute | solution.py:329
  112.8 29.9 %all-to-all-start.4 = ((bf16[16,64,576]{2,1,0:T(8,128)(2,1)}), bf16[16,64,576]{2,1,0:T(8,128)(2,1)S(1)}, u32[]{:S(2)}, u32[]{:S(2)}) async-start(bf16[16,64,576]{2,1,0:T(8,128)(2,1)} %get-tuple-element.16), calls=%async_computation.4 | async-start | bytes 2621440 | tf_op jit(solution)/shard_map/all_to_all | solution.py:268
  128.7 0.8 copy-start.3
  129.6 14.1 %copy-start.4 = (bf16[576,512]{1,0:T(8,128)(2,1)S(1)}, bf16[576,512]{1,0:T(8,128)(2,1)}, u32[]{:S(2)}) copy-start(bf16[576,512]{1,0:T(8,128)(2,1)} %shard_map.82) | copy-start | bytes 1769476

commit v5 on v4

--- a/solution.py
+++ b/solution.py
@@ -206,9 +206,10 @@
                 scores = scores_ref[n, :, cols]
                 expons = jnp.exp2((scores - jnp.max(scores, axis=0, keepdims=True)) * (scale * LOG2E))
                 probs = expons * (1.0 / jnp.sum(expons, axis=0, keepdims=True))
-                delta = jnp.sum(probs * dprob, axis=0, keepdims=True)
-                dscore = probs * (dprob - delta)
-                probs_ref[n, :, cols] = probs.astype(bf16)
+                probs_low = probs.astype(bf16)
+                delta = jnp.sum(probs_low.astype(jnp.float32) * dprob, axis=0, keepdims=True)
+                dscore = (scale * probs) * (dprob - delta)
+                probs_ref[n, :, cols] = probs_low
                 dscores_ref[n, :, cols] = dscore.astype(bf16)
                 falls_ref[n, i] = jnp.broadcast_to(jnp.sum(dscore, axis=1, keepdims=True), (BUCKET, BUCKET))
         for n, (b, h) in enumerate(todo):
@@ -218,11 +219,11 @@
                 ).T
             q, k, g = (part_of(which, b, h) for which in (0, 1, 3))
             dscore_tall = jnp.concatenate([dscores_ref[n, :, :BUCKET], dscores_ref[n, :, BUCKET:]], axis=0)
-            dq = scale * dot(blocked(k), dscore_tall, 1, 0)
+            dq = dot(blocked(k), dscore_tall, 1, 0)
             fall = jnp.concatenate(
                 [jnp.broadcast_to(falls[i : i + 1], (head_dim, BUCKET)) for i in (2 * h, 2 * h + 1)], axis=0
             )
-            dk = scale * (dot(blocked(q), dscores_ref[n], 1, 1) - fall * k.astype(jnp.float32))
+            dk = dot(blocked(q), dscores_ref[n], 1, 1) - fall * k.astype(jnp.float32)
             dv = dot(blocked(g), probs_ref[n], 1, 1)
             for which, grad in enumerate((dq, dk, dv)):
                 at = which * feat + h * pair

time: 145 us -> 145 us (level)
  no operation moved by 1% of the time
where the time goes in v5:
time: 145 us
  blocking collectives  47.1 us (32%)
  waiting for transfers between devices  46.4 us (32%)
  starting transfers between devices  24.1 us (17%)
  Pallas kernels  23.4 us (16%)
  local copies, waits for them, and re-layouts  2.14 us (1%)
    all_to_all x2, blocking collectives, exchange(): lax.all_to_all(chunks, AXES, 0, 0, tiled=True, axis_index_groups=halves)  47.1 us
    all_to_all x3, waiting for transfers between devices, exchange(): lax.all_to_all(chunks, AXES, 0, 0, tiled=True, axis_index_groups=halves)  27.8 us
    all_to_all x3, starting transfers between devices, exchange(): lax.all_to_all(chunks, AXES, 0, 0, tiled=True, axis_index_groups=halves)  14 us
    pallas_call x1, Pallas kernels, on_device(): reply_own, reply_other = attend(codes, arrived_own, arrived_other)  12.4 us
    ppermute x1, waiting for transfers between devices, on_device(): summed = lax.ppermute(folded, AXES, across)  12.2 us
    ppermute x4, starting transfers between devices, on_device(): copies = [lax.ppermute(array, AXES, across) for array in arrays]  7.92 us
    ppermute x4, waiting for transfers between devices, on_device(): copies = [lax.ppermute(array, AXES, across) for array in arrays]  6.42 us
    pallas_call x1, Pallas kernels, on_device(): pack(0, 2 * group * rows * points * 4 * feat)(wanted, *arrays)  3.94 us
  transfers between devices with their start and end apart: 8, of which 5 were waited for; matrix products, arithmetic and copies ran while one was open for 0% of the time, Pallas kernels for 5%

profile of v5, /device:TPU:0, one launch (start us, length us, event | category | flops | bytes accessed | tf_op | source)
XLA Modules:
  0.0 144.8 jit_solution(2904791592161249887)
XLA Ops:
  0.6 0.0 copy-start.2
  0.7 0.7 copy-done.2
  1.3 1.3 shard_map.76
  2.7 6.3 %all-to-all-start = ((s32[16,8,128]{2,1,0:T(8,128)}), s32[16,8,128]{2,1,0:T(8,128)S(1)}, u32[]{:S(2)}, u32[]{:S(2)}) async-start(s32[16,8,128]{2,1,0:T(8,128)} %get-tuple-element.12), calls=%async_computation | async-start | bytes 131072 | tf_op jit(solution)/shard_map/all_to_all | solution.py:269
  9.0 0.0 copy-done.5
  9.0 4.0 %collective-permute-start = (bf16[192,512]{1,0:T(8,128)(2,1)S(1)}, bf16[192,512]{1,0:T(8,128)(2,1)}, u32[]{:S(2)}, u32[]{:S(2)}) collective-permute-start(bf16[192,512]{1,0:T(8,128)(2,1)S(1)} %copy-done.5), channel_id=1, source_target_pairs={{0,6},{1,7},{2,4},{3,5},{4,2},{5,3},{6,0},{7,1},{8,14},{9,15},{10,... | collective-permute-start | bytes 589832 | tf_op jit(solution)/shard_map/ppermute | solution.py:289
  13.0 0.0 copy-done.6
  13.0 0.1 collective-permute-start.1
  13.1 3.7 %collective-permute-start.2 = (bf16[192,512]{1,0:T(8,128)(2,1)}, bf16[192,512]{1,0:T(8,128)(2,1)}, u32[]{:S(2)}, u32[]{:S(2)}) collective-permute-start(bf16[192,512]{1,0:T(8,128)(2,1)} %v_ref.1), channel_id=1, source_target_pairs={{0,6},{1,7},{2,4},{3,5},{4,2},{5,3},{6,0},{7,1},{8,14},{9,15},{10,... | collective-permute-start | bytes 589832 | tf_op jit(solution)/shard_map/ppermute | solution.py:289
  16.8 0.1 collective-permute-start.3
  16.9 0.0 all-to-all-done.wanted_ref
  16.9 0.6 copy-done
  17.6 3.9 %shard_map.77 = bf16[16,64,768]{2,1,0:T(8,128)(2,1)} custom-call(s32[16,8,128]{2,1,0:T(8,128)} %copy-done, bf16[192,512]{1,0:T(8,128)(2,1)} %q_ref.1, bf16[192,512]{1,0:T(8,128)(2,1)} %k_ref.1, bf16[192,512]{1,0:T(8,128)(2,1)} %v_ref.1, bf16[192,512]{1,0:T(8,128)(2,1)} %g_ref.1), custom_call_target="tpu_custom_call" | custom-call | flops 805306368 | bytes 1572864 | tf_op jit(solution)/shard_map/pallas_call | solution.py:304
  21.5 4.0 %all-to-all-start.1 = ((bf16[16,64,768]{2,1,0:T(8,128)(2,1)}), bf16[16,64,768]{2,1,0:T(8,128)(2,1)S(1)}, u32[]{:S(2)}, u32[]{:S(2)}) async-start(bf16[16,64,768]{2,1,0:T(8,128)(2,1)} %shard_map.77), calls=%async_computation.1 | async-start | bytes 3145728 | tf_op jit(solution)/shard_map/all_to_all | solution.py:269
  25.5 0.0 collective-permute-done.q_ref
  25.5 0.0 collective-permute-done.1.k_ref
  25.5 2.6 %collective-permute-done.2.v_ref = bf16[192,512]{1,0:T(8,128)(2,1)} collective-permute-done((bf16[192,512]{1,0:T(8,128)(2,1)}, bf16[192,512]{1,0:T(8,128)(2,1)}, u32[]{:S(2)}, u32[]{:S(2)}) %collective-permute-start.2) | collective-permute-done | bytes 196640 | tf_op jit(solution)/shard_map/ppermute | solution.py:289
  28.1 3.8 %collective-permute-done.3.g_ref = bf16[192,512]{1,0:T(8,128)(2,1)} collective-permute-done((bf16[192,512]{1,0:T(8,128)(2,1)}, bf16[192,512]{1,0:T(8,128)(2,1)}, u32[]{:S(2)}, u32[]{:S(2)}) %collective-permute-start.3) | collective-permute-done | bytes 196640 | tf_op jit(solution)/shard_map/ppermute | solution.py:289
  31.9 3.9 %shard_map.78 = bf16[16,64,768]{2,1,0:T(8,128)(2,1)} custom-call(s32[16,8,128]{2,1,0:T(8,128)} %copy-done, bf16[192,512]{1,0:T(8,128)(2,1)} %collective-permute-done.q_ref, bf16[192,512]{1,0:T(8,128)(2,1)} %collective-permute-done.1.k_ref, bf16[192,512]{1,0:T(8,128)(2,1)} %collective-permute-done.2.v_ref, bf16[192,512]{1,0:T(8,128)(2,1)} %collective-permute-done.3.g_ref), custom_call_target="tpu_custom_call" | custom-call | flops 40000000000 | bytes 1572864 | tf_op jit(solution)/shard_map/pallas_call | solution.py:305
  35.9 14.6 %all-to-all-done.1.own_ref = bf16[16,64,768]{2,1,0:T(8,128)(2,1)S(1)} async-done(((bf16[16,64,768]{2,1,0:T(8,128)(2,1)}), bf16[16,64,768]{2,1,0:T(8,128)(2,1)S(1)}, u32[]{:S(2)}, u32[]{:S(2)}) %all-to-all-start.1) | async-done | bytes 1572896 | tf_op jit(solution)/shard_map/all_to_all | solution.py:269
  50.4 25.9 %all_to_all.25.other_ref = bf16[16,64,768]{2,1,0:T(8,128)(2,1)S(1)} all-to-all(bf16[16,64,768]{2,1,0:T(8,128)(2,1)} %shard_map.78), channel_id=1, replica_groups={{0,1,2,3,8,9,10,11,16,17,18,19,24,25,26,27},{4,5,6,7,12,13,14,15,20,21,..., dimensions={0} | all-to-all | bytes 3145728 | tf_op jit(solution)/shard_map/all_to_all | solution.py:269
  76.4 12.4 %shard_map.79 = (bf16[16,64,576]{2,1,0:T(8,128)(2,1)}, bf16[16,64,576]{2,1,0:T(8,128)(2,1)S(1)}) custom-call(s32[3,512]{1,0:T(4,128)S(1)} %get-tuple-element.13.codes_ref, bf16[16,64,768]{2,1,0:T(8,128)(2,1)S(1)} %all-to-all-done.1.own_ref, bf16[16,64,768]{2,1,0:T(8,128)(2,1)S(1)} %all_to_all.25.other_ref), custom_call_target="tpu_custom_call" | custom-call | flops 20000000000 | bytes 8000000 | tf_op jit(solution)/shard_map/pallas_call | solution.py:321
  88.8 21.2 %all_to_all.26.replies_ref = bf16[16,64,576]{2,1,0:T(8,128)(2,1)S(1)} all-to-all(bf16[16,64,576]{2,1,0:T(8,128)(2,1)S(1)} %get-tuple-element.14), channel_id=1, replica_groups={{0,1,2,3,8,9,10,11,16,17,18,19,24,25,26,27},{4,5,6,7,12,13,14,15,20,21,..., dimensions={0} | all-to-all | bytes 2359296 | tf_op jit(solution)/shard_map/all_to_all | solution.py:269
  110.0 0.9 shard_map.80
  110.9 2.2 %collective-permute-start.4 = (bf16[576,512]{1,0:T(8,128)(2,1)S(1)}, bf16[576,512]{1,0:T(8,128)(2,1)S(1)}, u32[]{:S(2)}, u32[]{:S(2)}) collective-permute-start(bf16[576,512]{1,0:T(8,128)(2,1)S(1)} %shard_map.80), channel_id=1, source_target_pairs={{0,6},{1,7},{2,4},{3,5},{4,2},{5,3},{6,0},{7,1},{8,14},{9,15},{10,... | collective-permute-start | bytes 1769480 | tf_op jit(solution)/shard_map/ppermute | solution.py:330
  113.1 3.7 %all-to-all-start.4 = ((bf16[16,64,576]{2,1,0:T(8,128)(2,1)}), bf16[16,64,576]{2,1,0:T(8,128)(2,1)S(1)}, u32[]{:S(2)}, u32[]{:S(2)}) async-start(bf16[16,64,576]{2,1,0:T(8,128)(2,1)} %get-tuple-element.16), calls=%async_computation.4 | async-start | bytes 2621440 | tf_op jit(solution)/shard_map/all_to_all | solution.py:269
  116.8 12.2 %collective-permute-done.4.in_ref = bf16[576,512]{1,0:T(8,128)(2,1)S(1)} collective-permute-done((bf16[576,512]{1,0:T(8,128)(2,1)S(1)}, bf16[576,512]{1,0:T(8,128)(2,1)S(1)}, u32[]{:S(2)}, u32[]{:S(2)}) %collective-permute-start.4) | collective-permute-done | bytes 589856 | tf_op jit(solution)/shard_map/ppermute | solution.py:330
  129.0 0.8 copy-done.3
  129.8 13.2 %all-to-all-done.4.replies_ref = bf16[16,64,576]{2,1,0:T(8,128)(2,1)S(1)} async-done(((bf16[16,64,576]{2,1,0:T(8,128)(2,1)}), bf16[16,64,576]{2,1,0:T(8,128)(2,1)S(1)}, u32[]{:S(2)}, u32[]{:S(2)}) %all-to-all-start.4) | async-done | bytes 1179680 | tf_op jit(solution)/shard_map/all_to_all | solution.py:269
  143.0 0.9 shard_map.81
  143.9 0.0 copy-done.4
  143.9 0.9 add_convert_fusion
  (8 shorter events, 0.0 us)
Async XLA Ops:
  0.6 0.7 copy-start.2
  1.3 7.6 %copy-start.5 = (bf16[192,512]{1,0:T(8,128)(2,1)S(1)}, bf16[192,512]{1,0:T(8,128)(2,1)}, u32[]{:S(2)}) copy-start(bf16[192,512]{1,0:T(8,128)(2,1)} %q_ref.1) | copy-start | bytes 589828
  1.3 11.7 %copy-start.6 = (bf16[192,512]{1,0:T(8,128)(2,1)S(1)}, bf16[192,512]{1,0:T(8,128)(2,1)}, u32[]{:S(2)}) copy-start(bf16[192,512]{1,0:T(8,128)(2,1)} %k_ref.1) | copy-start | bytes 589828
  2.7 14.2 %all-to-all-start = ((s32[16,8,128]{2,1,0:T(8,128)}), s32[16,8,128]{2,1,0:T(8,128)S(1)}, u32[]{:S(2)}, u32[]{:S(2)}) async-start(s32[16,8,128]{2,1,0:T(8,128)} %get-tuple-element.12), calls=%async_computation | async-start | bytes 131072 | tf_op jit(solution)/shard_map/all_to_all | solution.py:269
  9.0 16.5 %collective-permute-start = (bf16[192,512]{1,0:T(8,128)(2,1)S(1)}, bf16[192,512]{1,0:T(8,128)(2,1)}, u32[]{:S(2)}, u32[]{:S(2)}) collective-permute-start(bf16[192,512]{1,0:T(8,128)(2,1)S(1)} %copy-done.5), channel_id=1, source_target_pairs={{0,6},{1,7},{2,4},{3,5},{4,2},{5,3},{6,0},{7,1},{8,14},{9,15},{10,... | collective-permute-start | bytes 589832 | tf_op jit(solution)/shard_map/ppermute | solution.py:289
  13.0 12.5 %collective-permute-start.1 = (bf16[192,512]{1,0:T(8,128)(2,1)S(1)}, bf16[192,512]{1,0:T(8,128)(2,1)}, u32[]{:S(2)}, u32[]{:S(2)}) collective-permute-start(bf16[192,512]{1,0:T(8,128)(2,1)S(1)} %copy-done.6), channel_id=1, source_target_pairs={{0,6},{1,7},{2,4},{3,5},{4,2},{5,3},{6,0},{7,1},{8,14},{9,15},{10,... | collective-permute-start | bytes 589832 | tf_op jit(solution)/shard_map/ppermute | solution.py:289
  13.1 15.0 %collective-permute-start.2 = (bf16[192,512]{1,0:T(8,128)(2,1)}, bf16[192,512]{1,0:T(8,128)(2,1)}, u32[]{:S(2)}, u32[]{:S(2)}) collective-permute-start(bf16[192,512]{1,0:T(8,128)(2,1)} %v_ref.1), channel_id=1, source_target_pairs={{0,6},{1,7},{2,4},{3,5},{4,2},{5,3},{6,0},{7,1},{8,14},{9,15},{10,... | collective-permute-start | bytes 589832 | tf_op jit(solution)/shard_map/ppermute | solution.py:289
  16.8 15.1 %collective-permute-start.3 = (bf16[192,512]{1,0:T(8,128)(2,1)}, bf16[192,512]{1,0:T(8,128)(2,1)}, u32[]{:S(2)}, u32[]{:S(2)}) collective-permute-start(bf16[192,512]{1,0:T(8,128)(2,1)} %g_ref.1), channel_id=1, source_target_pairs={{0,6},{1,7},{2,4},{3,5},{4,2},{5,3},{6,0},{7,1},{8,14},{9,15},{10,... | collective-permute-start | bytes 589832 | tf_op jit(solution)/shard_map/ppermute | solution.py:289
  16.9 0.6 copy-start
  21.5 29.0 %all-to-all-start.1 = ((bf16[16,64,768]{2,1,0:T(8,128)(2,1)}), bf16[16,64,768]{2,1,0:T(8,128)(2,1)S(1)}, u32[]{:S(2)}, u32[]{:S(2)}) async-start(bf16[16,64,768]{2,1,0:T(8,128)(2,1)} %shard_map.77), calls=%async_computation.1 | async-start | bytes 3145728 | tf_op jit(solution)/shard_map/all_to_all | solution.py:269
  88.8 21.2 %copy-start.1 = (s32[16,8,128]{2,1,0:T(8,128)S(1)}, s32[16,8,128]{2,1,0:T(8,128)}, u32[]{:S(2)}) copy-start(s32[16,8,128]{2,1,0:T(8,128)} %copy-done) | copy-start | bytes 196612
  110.9 18.1 %collective-permute-start.4 = (bf16[576,512]{1,0:T(8,128)(2,1)S(1)}, bf16[576,512]{1,0:T(8,128)(2,1)S(1)}, u32[]{:S(2)}, u32[]{:S(2)}) collective-permute-start(bf16[576,512]{1,0:T(8,128)(2,1)S(1)} %shard_map.80), channel_id=1, source_target_pairs={{0,6},{1,7},{2,4},{3,5},{4,2},{5,3},{6,0},{7,1},{8,14},{9,15},{10,... | collective-permute-start | bytes 1769480 | tf_op jit(solution)/shard_map/ppermute | solution.py:330
  113.1 29.9 %all-to-all-start.4 = ((bf16[16,64,576]{2,1,0:T(8,128)(2,1)}), bf16[16,64,576]{2,1,0:T(8,128)(2,1)S(1)}, u32[]{:S(2)}, u32[]{:S(2)}) async-start(bf16[16,64,576]{2,1,0:T(8,128)(2,1)} %get-tuple-element.16), calls=%async_computation.4 | async-start | bytes 2621440 | tf_op jit(solution)/shard_map/all_to_all | solution.py:269
  129.0 0.8 copy-start.3
  129.8 14.1 %copy-start.4 = (bf16[576,512]{1,0:T(8,128)(2,1)S(1)}, bf16[576,512]{1,0:T(8,128)(2,1)}, u32[]{:S(2)}) copy-start(bf16[576,512]{1,0:T(8,128)(2,1)} %shard_map.82) | copy-start | bytes 1769476

commit v6 on v5

--- a/solution.py
+++ b/solution.py
@@ -130,8 +130,10 @@
     codes_ref,
     own_ref,
     other_ref,
+    result_ref,
+    out_other_ref,
     out_own_ref,
-    out_other_ref,
+    sem,
     feats_ref,
     grads_ref,
     scores_ref,
@@ -228,9 +230,14 @@
             for which, grad in enumerate((dq, dk, dv)):
                 at = which * feat + h * pair
                 grads_ref[at : at + pair, b * BUCKET : (b + 1) * BUCKET] = grad.astype(bf16)
-        back = dot(picks, grads_ref[...], 1, 1).astype(bf16).reshape(2, group, span, 3 * feat)
+        grads = grads_ref[...]
         for part, ref in enumerate((out_own_ref, out_other_ref)):
-            ref[:, low:high, :] = ref[:, low:high, :] + back[part]
+            back = dot(picks[part * group * span : (part + 1) * group * span], grads, 1, 1).astype(bf16)
+            ref[:, low:high, :] = ref[:, low:high, :] + back.reshape(group, span, 3 * feat)
+            if t == tables - 1 and part == 0:
+                copy = pltpu.make_async_copy(out_own_ref, result_ref, sem)
+                copy.start()
+    copy.wait()
 
 
 def call(kernel, out_shape, scratch=(), flops=0, moved=0, in_specs=None, out_specs=None, vmem_bytes=VMEM_BYTES):
@@ -306,7 +313,11 @@
     attend = call(
         functools.partial(attend_kernel, windows),
         (reply, reply),
+        in_specs=[vmem] * 3,
+        out_specs=(hbm, vmem),
         scratch=(
+            pltpu.VMEM(reply.shape, bf16),
+            pltpu.SemaphoreType.DMA,
             pltpu.VMEM((4 * feat, points), bf16),
             pltpu.VMEM((3 * feat, points), bf16),
             pltpu.VMEM((steps, BUCKET, 2 * BUCKET), jnp.float32),

time: 145 us -> 146 us (level)
  no operation moved by 1% of the time
where the time goes in v6:
time: 146 us; the launch traced here: 145 us
  blocking collectives  47.1 us (32%)
  waiting for transfers between devices  46.4 us (32%)
  starting transfers between devices  24.1 us (17%)
  Pallas kernels  23.6 us (16%)
  local copies, waits for them, and re-layouts  2.14 us (1%)
    all_to_all x2, blocking collectives, exchange(): lax.all_to_all(chunks, AXES, 0, 0, tiled=True, axis_index_groups=halves)  47.1 us
    all_to_all x3, waiting for transfers between devices, exchange(): lax.all_to_all(chunks, AXES, 0, 0, tiled=True, axis_index_groups=halves)  27.8 us
    all_to_all x3, starting transfers between devices, exchange(): lax.all_to_all(chunks, AXES, 0, 0, tiled=True, axis_index_groups=halves)  14 us
    pallas_call x1, Pallas kernels, on_device(): reply_own, reply_other = attend(codes, arrived_own, arrived_other)  12.7 us
    ppermute x1, waiting for transfers between devices, on_device(): summed = lax.ppermute(folded, AXES, across)  12.2 us
    ppermute x4, starting transfers between devices, on_device(): copies = [lax.ppermute(array, AXES, across) for array in arrays]  7.92 us
    ppermute x4, waiting for transfers between devices, on_device(): copies = [lax.ppermute(array, AXES, across) for array in arrays]  6.42 us
    pallas_call x1, Pallas kernels, on_device(): pack(0, 2 * group * rows * points * 4 * feat)(wanted, *arrays)  3.94 us
  transfers between devices with their start and end apart: 8, of which 5 were waited for; matrix products, arithmetic and copies ran while one was open for 0% of the time, Pallas kernels for 5%

profile of v6, /device:TPU:0, one launch (start us, length us, event | category | flops | bytes accessed | tf_op | source)
XLA Modules:
  0.0 145.1 jit_solution(15959190324715473560)
XLA Ops:
  0.6 0.0 copy-start.2
  0.7 0.7 copy-done.2
  1.3 1.3 shard_map.76
  2.7 6.3 %all-to-all-start = ((s32[16,8,128]{2,1,0:T(8,128)}), s32[16,8,128]{2,1,0:T(8,128)S(1)}, u32[]{:S(2)}, u32[]{:S(2)}) async-start(s32[16,8,128]{2,1,0:T(8,128)} %get-tuple-element.12), calls=%async_computation | async-start | bytes 131072 | tf_op jit(solution)/shard_map/all_to_all | solution.py:276
  9.0 0.0 copy-done.5
  9.0 4.0 %collective-permute-start = (bf16[192,512]{1,0:T(8,128)(2,1)S(1)}, bf16[192,512]{1,0:T(8,128)(2,1)}, u32[]{:S(2)}, u32[]{:S(2)}) collective-permute-start(bf16[192,512]{1,0:T(8,128)(2,1)S(1)} %copy-done.5), channel_id=1, source_target_pairs={{0,6},{1,7},{2,4},{3,5},{4,2},{5,3},{6,0},{7,1},{8,14},{9,15},{10,... | collective-permute-start | bytes 589832 | tf_op jit(solution)/shard_map/ppermute | solution.py:296
  13.0 0.0 copy-done.6
  13.0 0.1 collective-permute-start.1
  13.1 3.7 %collective-permute-start.2 = (bf16[192,512]{1,0:T(8,128)(2,1)}, bf16[192,512]{1,0:T(8,128)(2,1)}, u32[]{:S(2)}, u32[]{:S(2)}) collective-permute-start(bf16[192,512]{1,0:T(8,128)(2,1)} %v_ref.1), channel_id=1, source_target_pairs={{0,6},{1,7},{2,4},{3,5},{4,2},{5,3},{6,0},{7,1},{8,14},{9,15},{10,... | collective-permute-start | bytes 589832 | tf_op jit(solution)/shard_map/ppermute | solution.py:296
  16.8 0.1 collective-permute-start.3
  16.9 0.0 all-to-all-done.wanted_ref
  16.9 0.6 copy-done
  17.6 3.9 %shard_map.77 = bf16[16,64,768]{2,1,0:T(8,128)(2,1)} custom-call(s32[16,8,128]{2,1,0:T(8,128)} %copy-done, bf16[192,512]{1,0:T(8,128)(2,1)} %q_ref.1, bf16[192,512]{1,0:T(8,128)(2,1)} %k_ref.1, bf16[192,512]{1,0:T(8,128)(2,1)} %v_ref.1, bf16[192,512]{1,0:T(8,128)(2,1)} %g_ref.1), custom_call_target="tpu_custom_call" | custom-call | flops 805306368 | bytes 1572864 | tf_op jit(solution)/shard_map/pallas_call | solution.py:311
  21.5 4.0 %all-to-all-start.1 = ((bf16[16,64,768]{2,1,0:T(8,128)(2,1)}), bf16[16,64,768]{2,1,0:T(8,128)(2,1)S(1)}, u32[]{:S(2)}, u32[]{:S(2)}) async-start(bf16[16,64,768]{2,1,0:T(8,128)(2,1)} %shard_map.77), calls=%async_computation.1 | async-start | bytes 3145728 | tf_op jit(solution)/shard_map/all_to_all | solution.py:276
  25.5 0.0 collective-permute-done.q_ref
  25.5 0.0 collective-permute-done.1.k_ref
  25.5 2.6 %collective-permute-done.2.v_ref = bf16[192,512]{1,0:T(8,128)(2,1)} collective-permute-done((bf16[192,512]{1,0:T(8,128)(2,1)}, bf16[192,512]{1,0:T(8,128)(2,1)}, u32[]{:S(2)}, u32[]{:S(2)}) %collective-permute-start.2) | collective-permute-done | bytes 196640 | tf_op jit(solution)/shard_map/ppermute | solution.py:296
  28.1 3.8 %collective-permute-done.3.g_ref = bf16[192,512]{1,0:T(8,128)(2,1)} collective-permute-done((bf16[192,512]{1,0:T(8,128)(2,1)}, bf16[192,512]{1,0:T(8,128)(2,1)}, u32[]{:S(2)}, u32[]{:S(2)}) %collective-permute-start.3) | collective-permute-done | bytes 196640 | tf_op jit(solution)/shard_map/ppermute | solution.py:296
  31.9 3.9 %shard_map.78 = bf16[16,64,768]{2,1,0:T(8,128)(2,1)} custom-call(s32[16,8,128]{2,1,0:T(8,128)} %copy-done, bf16[192,512]{1,0:T(8,128)(2,1)} %collective-permute-done.q_ref, bf16[192,512]{1,0:T(8,128)(2,1)} %collective-permute-done.1.k_ref, bf16[192,512]{1,0:T(8,128)(2,1)} %collective-permute-done.2.v_ref, bf16[192,512]{1,0:T(8,128)(2,1)} %collective-permute-done.3.g_ref), custom_call_target="tpu_custom_call" | custom-call | flops 40000000000 | bytes 1572864 | tf_op jit(solution)/shard_map/pallas_call | solution.py:312
  35.9 14.6 %all-to-all-done.1.own_ref = bf16[16,64,768]{2,1,0:T(8,128)(2,1)S(1)} async-done(((bf16[16,64,768]{2,1,0:T(8,128)(2,1)}), bf16[16,64,768]{2,1,0:T(8,128)(2,1)S(1)}, u32[]{:S(2)}, u32[]{:S(2)}) %all-to-all-start.1) | async-done | bytes 1572896 | tf_op jit(solution)/shard_map/all_to_all | solution.py:276
  50.4 25.9 %all_to_all.25.other_ref = bf16[16,64,768]{2,1,0:T(8,128)(2,1)S(1)} all-to-all(bf16[16,64,768]{2,1,0:T(8,128)(2,1)} %shard_map.78), channel_id=1, replica_groups={{0,1,2,3,8,9,10,11,16,17,18,19,24,25,26,27},{4,5,6,7,12,13,14,15,20,21,..., dimensions={0} | all-to-all | bytes 3145728 | tf_op jit(solution)/shard_map/all_to_all | solution.py:276
  76.4 12.7 %shard_map.79 = (bf16[16,64,576]{2,1,0:T(8,128)(2,1)}, bf16[16,64,576]{2,1,0:T(8,128)(2,1)S(1)}) custom-call(s32[3,512]{1,0:T(4,128)S(1)} %get-tuple-element.13.codes_ref, bf16[16,64,768]{2,1,0:T(8,128)(2,1)S(1)} %all-to-all-done.1.own_ref, bf16[16,64,768]{2,1,0:T(8,128)(2,1)S(1)} %all_to_all.25.other_ref), custom_call_target="tpu_custom_call" | custom-call | flops 20000000000 | bytes 8000000 | tf_op jit(solution)/shard_map/pallas_call | solution.py:332
  89.1 0.0 copy-start.1
  89.1 21.2 %all_to_all.26.replies_ref = bf16[16,64,576]{2,1,0:T(8,128)(2,1)S(1)} all-to-all(bf16[16,64,576]{2,1,0:T(8,128)(2,1)S(1)} %get-tuple-element.14), channel_id=1, replica_groups={{0,1,2,3,8,9,10,11,16,17,18,19,24,25,26,27},{4,5,6,7,12,13,14,15,20,21,..., dimensions={0} | all-to-all | bytes 2359296 | tf_op jit(solution)/shard_map/all_to_all | solution.py:276
  110.3 0.9 shard_map.80
  111.2 2.2 %collective-permute-start.4 = (bf16[576,512]{1,0:T(8,128)(2,1)S(1)}, bf16[576,512]{1,0:T(8,128)(2,1)S(1)}, u32[]{:S(2)}, u32[]{:S(2)}) collective-permute-start(bf16[576,512]{1,0:T(8,128)(2,1)S(1)} %shard_map.80), channel_id=1, source_target_pairs={{0,6},{1,7},{2,4},{3,5},{4,2},{5,3},{6,0},{7,1},{8,14},{9,15},{10,... | collective-permute-start | bytes 1769480 | tf_op jit(solution)/shard_map/ppermute | solution.py:341
  113.4 3.7 %all-to-all-start.4 = ((bf16[16,64,576]{2,1,0:T(8,128)(2,1)}), bf16[16,64,576]{2,1,0:T(8,128)(2,1)S(1)}, u32[]{:S(2)}, u32[]{:S(2)}) async-start(bf16[16,64,576]{2,1,0:T(8,128)(2,1)} %get-tuple-element.16), calls=%async_computation.4 | async-start | bytes 2621440 | tf_op jit(solution)/shard_map/all_to_all | solution.py:276
  117.1 12.2 %collective-permute-done.4.in_ref = bf16[576,512]{1,0:T(8,128)(2,1)S(1)} collective-permute-done((bf16[576,512]{1,0:T(8,128)(2,1)S(1)}, bf16[576,512]{1,0:T(8,128)(2,1)S(1)}, u32[]{:S(2)}, u32[]{:S(2)}) %collective-permute-start.4) | collective-permute-done | bytes 589856 | tf_op jit(solution)/shard_map/ppermute | solution.py:341
  129.3 0.8 copy-done.3
  130.1 13.2 %all-to-all-done.4.replies_ref = bf16[16,64,576]{2,1,0:T(8,128)(2,1)S(1)} async-done(((bf16[16,64,576]{2,1,0:T(8,128)(2,1)}), bf16[16,64,576]{2,1,0:T(8,128)(2,1)S(1)}, u32[]{:S(2)}, u32[]{:S(2)}) %all-to-all-start.4) | async-done | bytes 1179680 | tf_op jit(solution)/shard_map/all_to_all | solution.py:276
  143.3 0.9 shard_map.81
  144.2 0.9 add_convert_fusion
  (8 shorter events, 0.0 us)
Async XLA Ops:
  0.6 0.7 copy-start.2
  1.3 7.6 %copy-start.5 = (bf16[192,512]{1,0:T(8,128)(2,1)S(1)}, bf16[192,512]{1,0:T(8,128)(2,1)}, u32[]{:S(2)}) copy-start(bf16[192,512]{1,0:T(8,128)(2,1)} %q_ref.1) | copy-start | bytes 589828
  1.3 11.7 %copy-start.6 = (bf16[192,512]{1,0:T(8,128)(2,1)S(1)}, bf16[192,512]{1,0:T(8,128)(2,1)}, u32[]{:S(2)}) copy-start(bf16[192,512]{1,0:T(8,128)(2,1)} %k_ref.1) | copy-start | bytes 589828
  2.7 14.2 %all-to-all-start = ((s32[16,8,128]{2,1,0:T(8,128)}), s32[16,8,128]{2,1,0:T(8,128)S(1)}, u32[]{:S(2)}, u32[]{:S(2)}) async-start(s32[16,8,128]{2,1,0:T(8,128)} %get-tuple-element.12), calls=%async_computation | async-start | bytes 131072 | tf_op jit(solution)/shard_map/all_to_all | solution.py:276
  9.0 16.5 %collective-permute-start = (bf16[192,512]{1,0:T(8,128)(2,1)S(1)}, bf16[192,512]{1,0:T(8,128)(2,1)}, u32[]{:S(2)}, u32[]{:S(2)}) collective-permute-start(bf16[192,512]{1,0:T(8,128)(2,1)S(1)} %copy-done.5), channel_id=1, source_target_pairs={{0,6},{1,7},{2,4},{3,5},{4,2},{5,3},{6,0},{7,1},{8,14},{9,15},{10,... | collective-permute-start | bytes 589832 | tf_op jit(solution)/shard_map/ppermute | solution.py:296
  13.0 12.5 %collective-permute-start.1 = (bf16[192,512]{1,0:T(8,128)(2,1)S(1)}, bf16[192,512]{1,0:T(8,128)(2,1)}, u32[]{:S(2)}, u32[]{:S(2)}) collective-permute-start(bf16[192,512]{1,0:T(8,128)(2,1)S(1)} %copy-done.6), channel_id=1, source_target_pairs={{0,6},{1,7},{2,4},{3,5},{4,2},{5,3},{6,0},{7,1},{8,14},{9,15},{10,... | collective-permute-start | bytes 589832 | tf_op jit(solution)/shard_map/ppermute | solution.py:296
  13.1 15.0 %collective-permute-start.2 = (bf16[192,512]{1,0:T(8,128)(2,1)}, bf16[192,512]{1,0:T(8,128)(2,1)}, u32[]{:S(2)}, u32[]{:S(2)}) collective-permute-start(bf16[192,512]{1,0:T(8,128)(2,1)} %v_ref.1), channel_id=1, source_target_pairs={{0,6},{1,7},{2,4},{3,5},{4,2},{5,3},{6,0},{7,1},{8,14},{9,15},{10,... | collective-permute-start | bytes 589832 | tf_op jit(solution)/shard_map/ppermute | solution.py:296
  16.8 15.1 %collective-permute-start.3 = (bf16[192,512]{1,0:T(8,128)(2,1)}, bf16[192,512]{1,0:T(8,128)(2,1)}, u32[]{:S(2)}, u32[]{:S(2)}) collective-permute-start(bf16[192,512]{1,0:T(8,128)(2,1)} %g_ref.1), channel_id=1, source_target_pairs={{0,6},{1,7},{2,4},{3,5},{4,2},{5,3},{6,0},{7,1},{8,14},{9,15},{10,... | collective-permute-start | bytes 589832 | tf_op jit(solution)/shard_map/ppermute | solution.py:296
  16.9 0.6 copy-start
  21.5 29.0 %all-to-all-start.1 = ((bf16[16,64,768]{2,1,0:T(8,128)(2,1)}), bf16[16,64,768]{2,1,0:T(8,128)(2,1)S(1)}, u32[]{:S(2)}, u32[]{:S(2)}) async-start(bf16[16,64,768]{2,1,0:T(8,128)(2,1)} %shard_map.77), calls=%async_computation.1 | async-start | bytes 3145728 | tf_op jit(solution)/shard_map/all_to_all | solution.py:276
  89.1 21.2 %copy-start.1 = (s32[16,8,128]{2,1,0:T(8,128)S(1)}, s32[16,8,128]{2,1,0:T(8,128)}, u32[]{:S(2)}) copy-start(s32[16,8,128]{2,1,0:T(8,128)} %copy-done) | copy-start | bytes 196612
  111.2 18.1 %collective-permute-start.4 = (bf16[576,512]{1,0:T(8,128)(2,1)S(1)}, bf16[576,512]{1,0:T(8,128)(2,1)S(1)}, u32[]{:S(2)}, u32[]{:S(2)}) collective-permute-start(bf16[576,512]{1,0:T(8,128)(2,1)S(1)} %shard_map.80), channel_id=1, source_target_pairs={{0,6},{1,7},{2,4},{3,5},{4,2},{5,3},{6,0},{7,1},{8,14},{9,15},{10,... | collective-permute-start | bytes 1769480 | tf_op jit(solution)/shard_map/ppermute | solution.py:341
  113.4 29.9 %all-to-all-start.4 = ((bf16[16,64,576]{2,1,0:T(8,128)(2,1)}), bf16[16,64,576]{2,1,0:T(8,128)(2,1)S(1)}, u32[]{:S(2)}, u32[]{:S(2)}) async-start(bf16[16,64,576]{2,1,0:T(8,128)(2,1)} %get-tuple-element.16), calls=%async_computation.4 | async-start | bytes 2621440 | tf_op jit(solution)/shard_map/all_to_all | solution.py:276
  129.3 0.8 copy-start.3
  130.1 14.1 %copy-start.4 = (bf16[576,512]{1,0:T(8,128)(2,1)S(1)}, bf16[576,512]{1,0:T(8,128)(2,1)}, u32[]{:S(2)}) copy-start(bf16[576,512]{1,0:T(8,128)(2,1)} %shard_map.82) | copy-start | bytes 1769476
